TPU v7x, 256 devices: a whole 4x4x8 slice. The times are simulated.
256 devices in a mesh: section: 8 (over z_lo, x), expert: 8 (over z_hi, core), dp: 4 (over y).
Axes of the slice: x: 4, y: 4, z: 8 (z_hi: 4, z_lo: 2; z = z_hi * 2 + z_lo), core: 2. Of those that a mesh axis runs over, the one named last changes fastest.
Arguments:
- layer_inputs: bfloat16 [4096, 3072], P(('expert', 'dp')), may hold values from -6 to 6
- out_grad: bfloat16 [4096, 3072], P(('expert', 'dp')), may hold values from -6 to 6
- routes: int32 [4096, 2], P(('expert', 'dp')), may hold values from 0 to 7, all different within a row; in each aligned block of 64 rows (0 to 63, 64 to 127, ...) at most 24 rows name the same one
- gates: float32 [4096, 2], P(('expert', 'dp')), may hold values from 0.2 to 1
- w_in: bfloat16 [8, 3072, 8192], P('expert', 'dp', 'section'), may hold values from -0.109375 to 0.109375
- w_out: bfloat16 [8, 8192, 3072], P('expert', 'section', 'dp'), may hold values from -0.0625 to 0.0625
Outputs:
- in_grads: bfloat16 [4096, 3072], P(('expert', 'dp'))
- grad_w_in: bfloat16 [8, 3072, 8192], P('expert', 'dp', 'section')
- grad_w_out: bfloat16 [8, 8192, 3072], P('expert', 'section', 'dp')
Inputs may be any that keep to these rules, and one draw needn't show every extreme that they name: `routes`: in each aligned block of 64 rows of tokens no expert is named more than 24 times.
All inputs are finite; a program needn't handle non-finite values.
Results may differ from a plain program's by a relative error of at most 0.02.
Values may be sent and summed in bfloat16 or wider, within the bound.
A program may use at most 128 MiB of HBM per device.

v0:
```python
import jax
import jax.numpy as jnp
from jax import lax
from jax.sharding import PartitionSpec as P

ROWS = 64


def silu_slope(preact):
    sigmoid_val = jax.nn.sigmoid(preact)
    return sigmoid_val * (1.0 + preact * (1.0 - sigmoid_val))


def slot_tables(route_rows, expert_count, capacity):
    flat_routes = route_rows.reshape(-1)
    onehot = (flat_routes[:, None] == jnp.arange(expert_count, dtype=jnp.int32)[None, :]).astype(
        jnp.int32
    )
    before = jnp.cumsum(onehot, axis=0) - onehot
    slot_index = jnp.sum(before * onehot, axis=1)
    target = (flat_routes * capacity + slot_index).reshape(-1, 2)
    places = jnp.arange(expert_count * capacity, dtype=jnp.int32)
    first = (places[:, None] == target[None, :, 0]).astype(jnp.bfloat16)
    second = (places[:, None] == target[None, :, 1]).astype(jnp.bfloat16)
    return (first, second)


def transpose_dot(left, right):
    return lax.dot_general(
        left, right, (((0,), (0,)), ((), ())), preferred_element_type=jnp.float32
    )


def right_dot(left, right):
    return lax.dot_general(
        left, right, (((1,), (1,)), ((), ())), preferred_element_type=jnp.float32
    )


def send_home(back, expert_count, capacity):
    width = back.shape[1]
    moved = lax.all_to_all(
        back.reshape(expert_count, capacity, width),
        "expert",
        split_axis=0,
        concat_axis=0,
        tiled=True,
    )
    return moved.reshape(expert_count * capacity, width)


def on_device(layer_inputs, out_grad, routes, gates, w_in, w_out):
    expert_count = lax.axis_size("expert")
    tok_dev = layer_inputs.shape[0]
    width = layer_inputs.shape[1]
    row_count = ROWS
    micro_count = tok_dev // row_count
    capacity = 3 * row_count // expert_count
    slot_total = expert_count * capacity
    w_in_local = w_in[0]
    w_out_local = w_out[0]
    hid_width = w_in_local.shape[1]
    w_in_full, w_out_full = (
        lax.all_gather(w_in_local, "dp", axis=0, tiled=True),
        lax.all_gather(w_out_local, "dp", axis=1, tiled=True),
    )
    acc_in = jnp.zeros((width, hid_width), jnp.float32)
    acc_out = jnp.zeros((hid_width, width), jnp.float32)
    results = []
    for micro in range(micro_count):
        low = micro * row_count
        token_block = layer_inputs[low : low + row_count]
        upstream_wide = out_grad[low : low + row_count].astype(jnp.float32)
        route_rows = routes[low : low + row_count]
        gate_rows = gates[low : low + row_count]
        first, second = slot_tables(route_rows, expert_count, capacity)
        scaled_one = (gate_rows[:, 0:1] * upstream_wide).astype(jnp.bfloat16)
        scaled_two = (gate_rows[:, 1:2] * upstream_wide).astype(jnp.bfloat16)
        send_rows = jnp.dot(first + second, token_block, preferred_element_type=jnp.float32).astype(
            jnp.bfloat16
        )
        send_grads = (
            jnp.dot(first, scaled_one, preferred_element_type=jnp.float32)
            + jnp.dot(second, scaled_two, preferred_element_type=jnp.float32)
        ).astype(jnp.bfloat16)
        rows_in, grads_got = (
            lax.all_to_all(
                send_rows.reshape(expert_count, capacity, width),
                "expert",
                split_axis=0,
                concat_axis=0,
                tiled=True,
            ),
            lax.all_to_all(
                send_grads.reshape(expert_count, capacity, width),
                "expert",
                split_axis=0,
                concat_axis=0,
                tiled=True,
            ),
        )
        token_rows = rows_in.reshape(slot_total, width)
        grad_rows = grads_got.reshape(slot_total, width)
        preact = jnp.dot(token_rows, w_in_full, preferred_element_type=jnp.float32)
        hidden = jax.nn.silu(preact).astype(jnp.bfloat16)
        hidden_grad = right_dot(grad_rows, w_out_full)
        preact_grad = (hidden_grad * silu_slope(preact)).astype(jnp.bfloat16)
        back_part = right_dot(preact_grad, w_in_full)
        acc_in = acc_in + transpose_dot(token_rows, preact_grad)
        acc_out = acc_out + transpose_dot(hidden, grad_rows)
        back = lax.psum(back_part.astype(jnp.bfloat16), "section")
        returned = send_home(back, expert_count, capacity)
        contrib_one = transpose_dot(first, returned)
        contrib_two = transpose_dot(second, returned)
        results.append((upstream_wide + contrib_one + contrib_two).astype(jnp.bfloat16))
    in_grads = jnp.concatenate(results, axis=0)
    grad_one, grad_two = (
        lax.psum_scatter(acc_in.astype(jnp.bfloat16), "dp", scatter_dimension=0, tiled=True).astype(
            jnp.float32
        ),
        lax.psum_scatter(
            acc_out.astype(jnp.bfloat16), "dp", scatter_dimension=1, tiled=True
        ).astype(jnp.float32),
    )
    grad_w_in = grad_one.astype(jnp.bfloat16)[None]
    grad_w_out = grad_two.astype(jnp.bfloat16)[None]
    return (in_grads, grad_w_in, grad_w_out)


def solution(mesh):
    return jax.shard_map(
        on_device,
        mesh=mesh,
        in_specs=(
            P(("expert", "dp"), None),
            P(("expert", "dp"), None),
            P(("expert", "dp"), None),
            P(("expert", "dp"), None),
            P("expert", "dp", "section"),
            P("expert", "section", "dp"),
        ),
        out_specs=(
            P(("expert", "dp"), None),
            P("expert", "dp", "section"),
            P("expert", "section", "dp"),
        ),
        check_vma=False,
    )
```

profile of v0, /device:TPU:1, one launch (start us, length us, event | category | flops | bytes accessed | tf_op | source)
XLA Modules:
  0.0 411.6 jit_solution(5986060020042329236)
XLA Ops:
  7.2 0.7 all-gather.7.cloned.1.call-update
  8.0 0.7 all-gather.5.cloned.1.call-update
  8.8 0.1 copy.13
  8.8 0.1 eq.91
  9.1 0.2 reduce_window_sum.17
  9.3 0.2 select_reduce_fusion.1
  9.4 0.1 reduce_sum.23
  9.6 0.2 slice_reduce_fusion.2
  9.8 1.5 convolution_convert_fusion.1
  11.3 10.0 %all-to-all-start.1 = ((bf16[8,24,3072]{2,1,0:T(8,128)(2,1)}), bf16[8,24,3072]{2,1,0:T(8,128)(2,1)S(1)}, u32[]{:S(2)}, u32[]{:S(2)}) async-start(bf16[8,24,3072]{2,1,0:T(8,128)(2,1)} %bitcast.5), calls=%async_computation.1 | async-start | bytes 2359296 | tf_op jit(solution)/shard_map/all_to_all | solution.py:87
  21.3 0.1 eq.103
  21.5 0.2 reduce_window_sum.18
  21.7 0.2 select_reduce_fusion
  21.9 0.1 reduce_sum.25
  22.1 0.2 slice_reduce_fusion
  22.2 1.5 convolution_convert_fusion
  23.7 24.5 %all-to-all-done.1 = bf16[8,24,3072]{2,1,0:T(8,128)(2,1)S(1)} async-done(((bf16[8,24,3072]{2,1,0:T(8,128)(2,1)}), bf16[8,24,3072]{2,1,0:T(8,128)(2,1)S(1)}, u32[]{:S(2)}, u32[]{:S(2)}) %all-to-all-start.1) | async-done | bytes 1179680 | tf_op jit(solution)/shard_map/all_to_all | solution.py:87
  48.2 8.8 %all-to-all-start.4 = ((bf16[8,24,3072]{2,1,0:T(8,128)(2,1)}), bf16[8,24,3072]{2,1,0:T(8,128)(2,1)S(1)}, u32[]{:S(2)}, u32[]{:S(2)}) async-start(bf16[8,24,3072]{2,1,0:T(8,128)(2,1)} %bitcast.72), calls=%async_computation.4 | async-start | bytes 2359296 | tf_op jit(solution)/shard_map/all_to_all | solution.py:87
  57.0 0.5 fusion.43
  57.5 1.5 fusion.18
  59.1 25.0 %all-to-all-done.4 = bf16[8,24,3072]{2,1,0:T(8,128)(2,1)S(1)} async-done(((bf16[8,24,3072]{2,1,0:T(8,128)(2,1)}), bf16[8,24,3072]{2,1,0:T(8,128)(2,1)S(1)}, u32[]{:S(2)}, u32[]{:S(2)}) %all-to-all-start.4) | async-done | bytes 1179680 | tf_op jit(solution)/shard_map/all_to_all | solution.py:87
  84.1 9.1 %all-to-all-start = ((bf16[8,24,3072]{2,1,0:T(8,128)(2,1)}), bf16[8,24,3072]{2,1,0:T(8,128)(2,1)}, u32[]{:S(2)}, u32[]{:S(2)}) async-start(bf16[8,24,3072]{2,1,0:T(8,128)(2,1)} %bitcast.76), calls=%async_computation | async-start | bytes 2359296 | tf_op jit(solution)/shard_map/all_to_all | solution.py:94
  93.2 0.5 fusion.40
  93.7 1.5 fusion.19
  95.2 24.8 %all-to-all-done = bf16[8,24,3072]{2,1,0:T(8,128)(2,1)} async-done(((bf16[8,24,3072]{2,1,0:T(8,128)(2,1)}), bf16[8,24,3072]{2,1,0:T(8,128)(2,1)}, u32[]{:S(2)}, u32[]{:S(2)}) %all-to-all-start) | async-done | bytes 1179680 | tf_op jit(solution)/shard_map/all_to_all | solution.py:94
  120.0 9.5 %all-to-all-start.3 = ((bf16[8,24,3072]{2,1,0:T(8,128)(2,1)}), bf16[8,24,3072]{2,1,0:T(8,128)(2,1)}, u32[]{:S(2)}, u32[]{:S(2)}) async-start(bf16[8,24,3072]{2,1,0:T(8,128)(2,1)} %bitcast.75), calls=%async_computation.3 | async-start | bytes 2359296 | tf_op jit(solution)/shard_map/all_to_all | solution.py:94
  129.6 5.1 %fusion.6 = f32[192,1024]{1,0:T(8,128)} fusion(bf16[192,3072]{1,0:T(8,128)(2,1)S(1)} %bitcast.68, bf16[1,3072,1024]{2,1,0:T(8,128)(2,1)} %all-gather.7.cloned.1.call-done), kind=kOutput, calls=%fused_computation.8 | convolution fusion | flops 1207959552 | bytes 8257536 | tf_op jit(solution)/shard_map/dot_general | solution.py:104
  134.6 18.0 %all-gather.5.cloned.1.call-done = bf16[1,1024,3072]{2,1,0:T(8,128)(2,1)} async-done(((bf16[1,1024,768]{2,1,0:T(8,128)(2,1)}), bf16[1,1024,3072]{2,1,0:T(8,128)(2,1)}) %all-gather.5.cloned.1.call-update) | async-done | bytes 6291472 | tf_op jit(solution)/shard_map/all_gather | solution.py:65
  152.7 5.7 %fusion.31 = bf16[192,1024]{1,0:T(8,128)(2,1)S(1)} fusion(bf16[192,3072]{1,0:T(8,128)(2,1)} %bitcast.3, bf16[1,1024,3072]{2,1,0:T(8,128)(2,1)} %all-gather.5.cloned.1.call-done, f32[192,1024]{1,0:T(8,128)} %fusion.6), kind=kOutput, calls=%fused_computation.31 | convolution fusion | flops 1209729024 | bytes 8650752 | tf_op jit(solution)/shard_map/dot_general | solution.py:35
  158.4 3.3 fusion.12
  161.7 2.3 fusion.2
  164.1 5.6 %fusion.28 = bf16[192,1024]{1,0:T(8,128)(2,1)S(1)} fusion(bf16[192,3072]{1,0:T(8,128)(2,1)} %bitcast.13, bf16[1,1024,3072]{2,1,0:T(8,128)(2,1)} %all-gather.5.cloned.1.call-done, f32[192,1024]{1,0:T(8,128)} %fusion.2), kind=kOutput, calls=%fused_computation.30 | convolution fusion | flops 1209729024 | bytes 8650752 | tf_op jit(solution)/shard_map/dot_general | solution.py:35
  169.6 6.2 %fusion.15 = bf16[192,3072]{1,0:T(8,128)(2,1)} fusion(bf16[192,1024]{1,0:T(8,128)(2,1)S(1)} %fusion.28, bf16[1,3072,1024]{2,1,0:T(8,128)(2,1)} %all-gather.7.cloned.1.call-done), kind=kOutput, calls=%fused_computation.17 | convolution fusion | flops 1208549376 | bytes 7864320 | tf_op jit(solution)/shard_map/dot_general | solution.py:35
  175.9 0.3 reduce-scatter.5.cloned.1.call-start
  176.2 3.4 fusion.38
  179.6 5.9 %add_convert_fusion = bf16[1024,3072]{1,0:T(8,128)(2,1)} fusion(f32[1024,3072]{1,0:T(8,128)S(1)} %fusion.38, bf16[192,3072]{1,0:T(8,128)(2,1)} %bitcast.13, f32[192,1024]{1,0:T(8,128)S(1)} %copy-done.4), kind=kOutput, calls=%fused_computation | convolution fusion | flops 1215234048 | bytes 20840448 | tf_op jit(solution)/shard_map/dot_general | solution.py:29
  185.6 1.8 fusion.84
  187.4 4.6 %add_convert_fusion.1 = bf16[3072,1024]{1,0:T(8,128)(2,1)} fusion(f32[3072,1024]{1,0:T(8,128)S(1)} %fusion.84, bf16[192,3072]{1,0:T(8,128)(2,1)S(1)} %bitcast.71, bf16[192,1024]{1,0:T(8,128)(2,1)S(1)} %copy-done.3), kind=kOutput, calls=%fused_computation.1 | convolution fusion | flops 1214251008 | bytes 20447232 | tf_op jit(solution)/shard_map/dot_general | solution.py:29
  192.0 70.7 %all-reduce.3.cloned.1.call-done = (bf16[8,24,3072]{2,1,0:T(8,128)(2,1)}, bf16[8,24,3072]{2,1,0:T(8,128)(2,1)}) async-done(((bf16[8,24,3072]{2,1,0:T(8,128)(2,1)}, bf16[8,24,3072]{2,1,0:T(8,128)(2,1)}), (bf16[8,24,3072]{2,1,0:T(8,128)(2,1)}, bf16[8,24,3072]{2,1,0:T(8,128)(2,1)})) %all-reduce.3.cloned.1.call-update) | async-done | bytes 2359312 | tf_op jit(solution)/shard_map/psum | solution.py:111
  262.7 36.1 %all_to_all.30 = bf16[8,24,3072]{2,1,0:T(8,128)(2,1)S(1)} all-to-all(bf16[8,24,3072]{2,1,0:T(8,128)(2,1)} %get-tuple-element.8), channel_id=1, replica_groups=mesh['section'=8,'expert'=8,'dp'=4] {'expert'}, dimensions={0} | all-to-all | bytes 2359296 | tf_op jit(solution)/shard_map/all_to_all | solution.py:42
  298.8 9.9 %all-to-all-start.5 = ((bf16[8,24,3072]{2,1,0:T(8,128)(2,1)}), bf16[8,24,3072]{2,1,0:T(8,128)(2,1)S(1)}, u32[]{:S(2)}, u32[]{:S(2)}) async-start(bf16[8,24,3072]{2,1,0:T(8,128)(2,1)} %get-tuple-element.7), calls=%async_computation.5 | async-start | bytes 2359296 | tf_op jit(solution)/shard_map/all_to_all | solution.py:42
  308.7 0.4 convolution_add_fusion.5
  309.1 0.4 fusion.20
  309.5 28.4 %all-to-all-done.5 = bf16[8,24,3072]{2,1,0:T(8,128)(2,1)S(1)} async-done(((bf16[8,24,3072]{2,1,0:T(8,128)(2,1)}), bf16[8,24,3072]{2,1,0:T(8,128)(2,1)S(1)}, u32[]{:S(2)}, u32[]{:S(2)}) %all-to-all-start.5) | async-done | bytes 1179680 | tf_op jit(solution)/shard_map/all_to_all | solution.py:42
  337.8 0.4 convolution_add_fusion.3
  338.2 0.4 fusion.21
  338.6 0.9 pad_maximum_fusion
  339.5 65.5 %reduce-scatter.3.cloned.1.call-done = bf16[768,1024]{1,0:T(8,128)(2,1)} async-done(((bf16[3072,1024]{1,0:T(8,128)(2,1)}), bf16[768,1024]{1,0:T(8,128)(2,1)}) %reduce-scatter.3.cloned.1.call-update) | async-done | bytes 1572880 | tf_op jit(solution)/shard_map/reduce_scatter | solution.py:118
  (33 shorter events, 0.6 us)
Async XLA Ops:
  7.2 1.5 copy-start.6
  7.2 122.4 %all-gather.7.cloned.1.call-start = ((), (), s32[]{:S(2)}) async-start(), calls=%async_computation.11 | async-start | bytes 7864320 | tf_op jit(solution)/shard_map/all_gather | solution.py:64
  7.9 1.9 copy-start.5
  7.9 144.7 %all-gather.5.cloned.1.call-start = ((), (), s32[]{:S(2)}) async-start(), calls=%async_computation.10 | async-start | bytes 7864320 | tf_op jit(solution)/shard_map/all_gather | solution.py:65
  11.3 36.9 %all-to-all-start.1 = ((bf16[8,24,3072]{2,1,0:T(8,128)(2,1)}), bf16[8,24,3072]{2,1,0:T(8,128)(2,1)S(1)}, u32[]{:S(2)}, u32[]{:S(2)}) async-start(bf16[8,24,3072]{2,1,0:T(8,128)(2,1)} %bitcast.5), calls=%async_computation.1 | async-start | bytes 2359296 | tf_op jit(solution)/shard_map/all_to_all | solution.py:87
  48.2 8.8 %copy-start.7 = (f32[128,2]{0,1:T(2,128)S(1)}, f32[128,2]{0,1:T(2,128)}, u32[]{:S(2)}) copy-start(f32[128,2]{0,1:T(2,128)} %param.9) | copy-start | bytes 3076
  48.2 8.9 %copy-start.1 = (bf16[128,3072]{1,0:T(8,128)(2,1)S(1)}, bf16[128,3072]{1,0:T(8,128)(2,1)}, u32[]{:S(2)}) copy-start(bf16[128,3072]{1,0:T(8,128)(2,1)} %param.7) | copy-start | bytes 2359300
  48.2 35.9 %all-to-all-start.4 = ((bf16[8,24,3072]{2,1,0:T(8,128)(2,1)}), bf16[8,24,3072]{2,1,0:T(8,128)(2,1)S(1)}, u32[]{:S(2)}, u32[]{:S(2)}) async-start(bf16[8,24,3072]{2,1,0:T(8,128)(2,1)} %bitcast.72), calls=%async_computation.4 | async-start | bytes 2359296 | tf_op jit(solution)/shard_map/all_to_all | solution.py:87
  84.1 36.0 %all-to-all-start = ((bf16[8,24,3072]{2,1,0:T(8,128)(2,1)}), bf16[8,24,3072]{2,1,0:T(8,128)(2,1)}, u32[]{:S(2)}, u32[]{:S(2)}) async-start(bf16[8,24,3072]{2,1,0:T(8,128)(2,1)} %bitcast.76), calls=%async_computation | async-start | bytes 2359296 | tf_op jit(solution)/shard_map/all_to_all | solution.py:94
  120.0 44.0 %all-to-all-start.3 = ((bf16[8,24,3072]{2,1,0:T(8,128)(2,1)}), bf16[8,24,3072]{2,1,0:T(8,128)(2,1)}, u32[]{:S(2)}, u32[]{:S(2)}) async-start(bf16[8,24,3072]{2,1,0:T(8,128)(2,1)} %bitcast.75), calls=%async_computation.3 | async-start | bytes 2359296 | tf_op jit(solution)/shard_map/all_to_all | solution.py:94
  129.6 133.2 %all-reduce.3.cloned.1.call-start = ((), (), s32[]{:S(2)}) async-start(), calls=%async_computation.12 | async-start | bytes 4718592 | tf_op jit(solution)/shard_map/psum | solution.py:111
  152.7 5.7 %copy-start = (bf16[1,3072,1024]{2,1,0:T(8,128)(2,1)S(1)}, bf16[1,3072,1024]{2,1,0:T(8,128)(2,1)}, u32[]{:S(2)}) copy-start(bf16[1,3072,1024]{2,1,0:T(8,128)(2,1)} %all-gather.7.cloned.1.call-done) | copy-start | bytes 18874372
  169.6 6.2 %copy-start.2 = (bf16[192,1024]{1,0:T(8,128)(2,1)}, bf16[192,1024]{1,0:T(8,128)(2,1)S(1)}, u32[]{:S(2)}) copy-start(bf16[192,1024]{1,0:T(8,128)(2,1)S(1)} %fusion.28) | copy-start | bytes 1179652
  175.9 163.7 %reduce-scatter.5.cloned.1.call-start = ((), (), s32[]{:S(2)}) async-start(), calls=%async_computation.9 | async-start | bytes 7864320 | tf_op jit(solution)/shard_map/reduce_scatter | solution.py:121
  176.1 3.5 copy-start.4
  185.5 219.6 %reduce-scatter.3.cloned.1.call-start = ((), (), s32[]{:S(2)}) async-start(), calls=%async_computation.8 | async-start | bytes 7864320 | tf_op jit(solution)/shard_map/reduce_scatter | solution.py:118
  185.6 1.8 copy-start.3
  298.8 39.1 %all-to-all-start.5 = ((bf16[8,24,3072]{2,1,0:T(8,128)(2,1)}), bf16[8,24,3072]{2,1,0:T(8,128)(2,1)S(1)}, u32[]{:S(2)}, u32[]{:S(2)}) async-start(bf16[8,24,3072]{2,1,0:T(8,128)(2,1)} %get-tuple-element.7), calls=%async_computation.5 | async-start | bytes 2359296 | tf_op jit(solution)/shard_map/all_to_all | solution.py:42
Sparse Core Ops, SparseCore 0:
  9.8 72.0 all-gather.6
  83.7 68.9 all-gather.4
  176.0 86.6 all-reduce.2
  265.7 70.0 reduce-scatter.4
  338.8 66.2 reduce-scatter.2
where the time goes:
time: 412 us
  waiting for transfers between devices  258 us (63%)
  matrix products  52.5 us (13%)
  starting transfers between devices  47.6 us (12%)
  blocking collectives  36.1 us (9%)
  between operations  14 us (3%)
    psum x1, waiting for transfers between devices, on_device(): back = lax.psum(back_part.astype(jnp.bfloat16), 'section')  70.7 us
    reduce_scatter x1, waiting for transfers between devices, on_device(): lax.psum_scatter(acc_in.astype(jnp.bfloat16), 'dp', scatter_dimension=0,...  65.5 us
    all_to_all x2, waiting for transfers between devices, on_device(): lax.all_to_all(send_rows.reshape(expert_count, capacity, width), 'expert'...  49.4 us
    all_to_all x1, blocking collectives, send_home(): lax.all_to_all(back.reshape(expert_count, capacity, width), 'expert', spl...  36.1 us
    all_to_all x1, waiting for transfers between devices, send_home(): lax.all_to_all(back.reshape(expert_count, capacity, width), 'expert', spl...  28.4 us
    all_to_all x2, waiting for transfers between devices, on_device(): lax.all_to_all(send_grads.reshape(expert_count, capacity, width), 'expert...  24.8 us
    dot_general x4, matrix products, right_dot(): lax.dot_general(left, right, (((1,), (1,)), ((), ())), preferred_element_...  20.8 us
    all_to_all x2, starting transfers between devices, on_device(): lax.all_to_all(send_rows.reshape(expert_count, capacity, width), 'expert'...  18.7 us
  transfers between devices with their start and end apart: 10, of which 7 were waited for; matrix products, arithmetic and copies ran while one was open for 11% of the time, Pallas kernels for 0%

commit v1 on v0

v1 whole, which is shorter than its diff:
```python
import jax
import jax.numpy as jnp
from jax import lax
from jax.experimental import pallas as pl
from jax.experimental.pallas import tpu as pltpu
from jax.sharding import PartitionSpec as P

MESH = pl.DeviceIdType.MESH
F32 = jnp.float32
BF16 = jnp.bfloat16

ROWS = 64
NX = 4
NY = 4
NZ = 4
SLOTS = 48
D_LOC = 768
HALF = D_LOC // 2
F_LOC = 1024
TILE = 256

FROM_Z = (0, 1, 3, 2)
A2A, BZ, B_OWN, B_OTHER, B_FWD = 0, 2, 3, 5, 7
R_FAR, R_NEAR, R_SUM = 9, 11, 13
G_OWN, G_FWD = 15, 17
PART = 19
S_FAR, S_NEAR, S_SUM, S_Z = 38, 40, 42, 44
HOME = 45
COPIES = 47
O_Z, O_OWN, O_OTHER, O_FWD = 0, 1, 3, 5
OUT_COPIES = 7
PLAN = (
    "s00", "s01", "a00", "b00", "s10", "c00", "a01", "b01", "s11", "d00", "c01", "a10", "b10", "s20",
    "s21", "e00", "d01", "c10", "a11", "b11", "e01", "d10", "c11", "s30", "s31", "a20", "b20", "f0",
    "e10", "d11", "c20", "a21", "b21", "g0", "e11", "d20", "c21", "a30", "b30", "f1", "e20", "d21",
    "c30", "a31", "b31", "g1", "h0", "e21", "d30", "c31", "f2", "e30", "d31", "g2", "h1", "i0",
    "e31", "f3", "i1", "j0", "h2", "g3", "o0", "o1", "o2", "o3", "j1", "l0", "i2", "h3",
    "l1", "j2", "u0", "i3", "l2", "u1", "j3", "u2", "l3", "q0", "w0", "q1", "w1", "q2",
    "w2", "q3", "v0", "v1", "v2", "v3", "x0", "x1", "x2", "x3", "w3",
)


def kernel(
    x_ref,
    up_ref,
    routes_ref,
    gates_ref,
    w_in_ref,
    w_out_ref,
    ing_ref,
    gin_ref,
    gout_ref,
    xg,
    ps,
    r1,
    r2,
    hp,
    bk,
    q1,
    q2,
    q3,
    rb,
    ret,
    ssem,
    rsem,
    osend,
    orecv,
    lsem,
    w_in,
    w_out,
    gin,
    gout,
    ing,
    acc,
    xs,
    us,
    send,
    comb,
):
    section = lax.axis_index("section")
    expert = lax.axis_index("expert")
    y = lax.axis_index("dp")
    x, c = lax.rem(section, NX), section // NX
    zh, core = expert // 2, lax.rem(expert, 2)

    def around(value, n=4):
        return lax.rem(value + 2 * n, n)

    x_dev = (
        {"section": c * NX + around(x + 1)},
        {"section": c * NX + around(x - 1)},
    )
    z_dev = {"section": (1 - c) * NX + x}
    y_dev = ({"dp": around(y + 1)}, {"dp": around(y - 1)})
    y_to = around(y - x)
    y_from = around(y + x)
    to_cols = pl.ds(pl.multiple_of(y_to * D_LOC + c * HALF, 128), HALF)
    mine = pl.ds(pl.multiple_of(c * HALF, 128), HALF)
    other = pl.ds(pl.multiple_of((1 - c) * HALF, 128), HALF)

    def load(n):
        src, dst = (
            (w_in_ref, w_in),
            (w_out_ref, w_out),
            (x_ref.at[:, to_cols], xs),
            (up_ref.at[:, to_cols], us),
        )[n]
        return pltpu.make_async_copy(src, dst, lsem.at[n])

    for n in (2, 3, 0, 1):
        load(n).start()
    stores = []

    def store(src, dst, rows, n):
        copy = pltpu.make_async_copy(src.at[rows], dst.at[rows], lsem.at[4 + n])
        copy.start()
        stores.append(copy)

    barrier = pltpu.get_barrier_semaphore()
    for dev in x_dev + y_dev + (z_dev,):
        pl.semaphore_signal(barrier, inc=1, device_id=dev, device_id_type=MESH)
    for e in range(2 * NZ):
        for yy in (y_to, y_from):

            @pl.when(jnp.logical_or(x != 0, expert != e))
            def _(e=e, yy=yy):
                pl.semaphore_signal(
                    barrier,
                    inc=1,
                    device_id={"expert": jnp.int32(e), "dp": yy},
                    device_id_type=MESH,
                )

    tokens, count = us.shape[0], 2 * NZ * SLOTS
    place = lax.broadcasted_iota(jnp.int32, (tokens, count), 1)
    expert_of = sum((place >= SLOTS * e).astype(jnp.int32) for e in range(1, 2 * NZ))
    token = lax.broadcasted_iota(jnp.int32, (tokens, count), 0)
    micro_start = jnp.where(token >= ROWS, SLOTS // 2, 0)
    is_first = routes_ref[:, 0:1] == expert_of
    is_second = routes_ref[:, 1:2] == expert_of
    named = jnp.logical_or(is_first, is_second)
    row = lax.broadcasted_iota(jnp.int32, (tokens, tokens), 0)
    col = lax.broadcasted_iota(jnp.int32, (tokens, tokens), 1)
    earlier = jnp.logical_and(col < row, col >= jnp.where(row >= ROWS, ROWS, 0))

    def ones(mask):
        return jnp.where(mask, 1.0, 0.0).astype(BF16)

    before = jnp.dot(ones(earlier), ones(named), preferred_element_type=F32)
    slot = (place - SLOTS * expert_of - micro_start).astype(F32)
    taken = jnp.logical_and(named, before == slot)
    comb[...] = ones(taken)

    def picked(mask, rows):
        return lax.dot_general(
            ones(mask), rows, (((0,), (0,)), ((), ())), preferred_element_type=F32
        )

    load(2).wait()
    send[0] = picked(taken, xs[...]).astype(BF16).reshape(2 * NZ, SLOTS, HALF)
    load(3).wait()
    wide = us[...].astype(F32)
    send[1] = (
        picked(jnp.logical_and(taken, is_first), (gates_ref[:, 0:1] * wide).astype(BF16))
        + picked(jnp.logical_and(taken, is_second), (gates_ref[:, 1:2] * wide).astype(BF16))
    ).astype(BF16).reshape(2 * NZ, SLOTS, HALF)

    pl.semaphore_wait(barrier, jnp.where(x == 0, 19, 21))

    sent = []

    def remote(src, dst, k, j, dev, rj=None):
        return pltpu.make_async_remote_copy(
            src_ref=src,
            dst_ref=dst,
            send_sem=ssem.at[k, j],
            recv_sem=rsem.at[k, j if rj is None else rj],
            device_id=dev,
            device_id_type=MESH,
        )

    def push(src, dst, k, j, dev, rj=None):
        copy = remote(src, dst, k, j, dev, rj)
        copy.start()
        sent.append(copy)

    def arrived(dst, k, j):
        remote(dst, dst, k, j, z_dev).wait_recv()

    def push_expert(src, dst, k, j, e, yy, rj):
        if k != 0:
            push(src, dst, k, j, {"expert": e, "dp": yy}, rj)
            return
        own = jnp.logical_and(x == 0, expert == e)
        copy = remote(src, dst, k, j, {"expert": e, "dp": yy}, rj)
        local = pltpu.make_async_copy(src, dst, rsem.at[k, rj])

        @pl.when(own)
        def _():
            local.start()

        @pl.when(jnp.logical_not(own))
        def _():
            copy.start()

        class Guarded:
            def wait_send(self):
                @pl.when(jnp.logical_not(own))
                def _():
                    copy.wait_send()

        sent.append(Guarded())

    def start_dispatch(k, m):
        zd = around(zh - FROM_Z[k])
        for to_core in range(2):
            e = zd * 2 + to_core
            push_expert(
                send.at[m, e],
                xg.at[m, k, y, core, :, mine],
                k,
                PART * m + A2A + to_core,
                e,
                y_to,
                PART * m + A2A + core,
            )

    def piece(k, m, dx, cols):
        return xg.at[m, k, around(y + x + dx), :, :, cols]

    def share(ref, k, j, dev):
        push(ref, ref, k, j, dev)

    def share_own(k, m):
        for b in range(2):
            arrived(xg.at[m, k, y_from, b, :, mine], k, PART * m + A2A + b)
        share(piece(k, m, 0, mine), k, PART * m + BZ, z_dev)
        for i in range(2):
            share(piece(k, m, 0, mine), k, PART * m + B_OWN + i, x_dev[i])

    def share_other(k, m):
        arrived(piece(k, m, 0, other), k, PART * m + BZ)
        for i in range(2):
            share(piece(k, m, 0, other), k, PART * m + B_OTHER + i, x_dev[i])

    def share_far(k, m):
        arrived(piece(k, m, -1, mine), k, PART * m + B_OWN)
        share(piece(k, m, -1, mine), k, PART * m + B_FWD, x_dev[0])
        arrived(piece(k, m, 1, other), k, PART * m + B_OTHER + 1)
        share(piece(k, m, 1, other), k, PART * m + B_FWD + 1, x_dev[1])

    def project(k, m):
        if k == 0:
            load(m).wait()
        arrived(piece(k, m, 1, mine), k, PART * m + B_OWN + 1)
        arrived(piece(k, m, -1, other), k, PART * m + B_OTHER)
        arrived(piece(k, m, 2, mine), k, PART * m + B_FWD)
        arrived(piece(k, m, 2, other), k, PART * m + B_FWD + 1)

        def body(n, _):
            cols = pl.ds(pl.multiple_of(n * TILE, TILE), TILE)
            rows = xg[m, k].reshape(NY * 2 * SLOTS, D_LOC)
            if m == 0:
                part = jnp.dot(rows, w_in[:, cols], preferred_element_type=F32)
            else:
                part = lax.dot_general(
                    rows, w_out[cols, :], (((1,), (1,)), ((), ())), preferred_element_type=F32
                )
            ps[k, m, :, :, :, cols] = part.astype(BF16).reshape(NY, 2, SLOTS, TILE)
            return 0

        lax.fori_loop(0, F_LOC // TILE, body, 0)
        far, after, before = (around(y + d) for d in (2, 1, -1))
        j = PART * m
        push(ps.at[k, m, far, 0], r1.at[k, m, 0], k, j + R_FAR, y_dev[0])
        push(ps.at[k, m, far, 1], r1.at[k, m, 1], k, j + R_FAR + 1, y_dev[1])
        push(ps.at[k, m, after, 1], r2.at[k, m, 0, 1], k, j + R_NEAR, y_dev[0])
        push(ps.at[k, m, before, 0], r2.at[k, m, 1, 0], k, j + R_NEAR + 1, y_dev[1])

    def pass_sums(k, m):
        for i in range(2):
            arrived(r1.at[k, m, i], k, PART * m + R_FAR + i)
            to = around(y + 1 - 2 * i)
            total = ps[k, m, to, i].astype(F32) + r1[k, m, i].astype(F32)
            ps[k, m, to, i] = total.astype(BF16)
            push(ps.at[k, m, to, i], r2.at[k, m, i, i], k, PART * m + R_SUM + i, y_dev[i])

    def activate(k):
        for m in range(2):
            for i in range(2):
                arrived(r2.at[k, m, i, 1 - i], k, PART * m + R_NEAR + i)
                arrived(r2.at[k, m, i, i], k, PART * m + R_SUM + i)
        for b in range(2):
            pre, grad = (
                ps[k, m, y, b].astype(F32)
                + r2[k, m, 0, b].astype(F32)
                + r2[k, m, 1, b].astype(F32)
                for m in range(2)
            )
            s = jax.nn.sigmoid(pre)
            hp[0, k, y, b] = (pre * s).astype(BF16)
            hp[1, k, y, b] = (grad * (s * (1.0 + pre * (1.0 - s)))).astype(BF16)
        gather_own(k, 1)

    def gather_own(k, m):
        for i in range(2):
            share(hp.at[m, k, y], k, PART * m + G_OWN + i, y_dev[i])

    def gather_far(k, m):
        for i in range(2):
            near = around(y - 1 + 2 * i)
            arrived(hp.at[m, k, near], k, PART * m + G_OWN + i)
            share(hp.at[m, k, near, i], k, PART * m + G_FWD + i, y_dev[i])

    def gathered(k, m):
        for i in range(2):
            arrived(hp.at[m, k, around(y + 2), i], k, PART * m + G_FWD + i)

    def go_back(k):
        gathered(k, 1)

        def body(n, _):
            cols = pl.ds(pl.multiple_of(n * TILE, TILE), TILE)
            part = lax.dot_general(
                hp[1, k].reshape(NY * 2 * SLOTS, F_LOC),
                w_in[cols, :],
                (((1,), (1,)), ((), ())),
                preferred_element_type=F32,
            )
            bk[k, :, :, :, cols] = part.astype(BF16).reshape(NY, 2, SLOTS, TILE)
            return 0

        lax.fori_loop(0, D_LOC // TILE, body, 0)
        far, after, before = (around(y + x + d) for d in (2, 1, -1))
        push(bk.at[k, far, 0], q1.at[k, 0], k, S_FAR, x_dev[0])
        push(bk.at[k, far, 1], q1.at[k, 1], k, S_FAR + 1, x_dev[1])
        push(bk.at[k, after, 1], q2.at[k, 0, 1], k, S_NEAR, x_dev[0])
        push(bk.at[k, before, 0], q2.at[k, 1, 0], k, S_NEAR + 1, x_dev[1])

    def back_sums(k):
        for i in range(2):
            arrived(q1.at[k, i], k, S_FAR + i)
            to = around(y + x + 1 - 2 * i)
            total = bk[k, to, i].astype(F32) + q1[k, i].astype(F32)
            bk[k, to, i] = total.astype(BF16)
            push(bk.at[k, to, i], q2.at[k, i, i], k, S_SUM + i, x_dev[i])

    def back_across(k):
        for i in range(2):
            arrived(q2.at[k, i, 1 - i], k, S_NEAR + i)
            arrived(q2.at[k, i, i], k, S_SUM + i)
        for b in range(2):
            total = (
                bk[k, y_from, b].astype(F32) + q2[k, 0, b].astype(F32) + q2[k, 1, b].astype(F32)
            )
            bk[k, y_from, b] = total.astype(BF16)
        push(bk.at[k, y_from, :, :, other], q3.at[k], k, S_Z, z_dev)

    def send_home(k):
        arrived(q3.at[k], k, S_Z)
        rb[k] = (bk[k, y_from, :, :, mine].astype(F32) + q3[k].astype(F32)).astype(BF16)
        zs = around(zh + FROM_Z[k])
        for to_core in range(2):
            push_expert(
                rb.at[k, to_core],
                ret.at[expert],
                k,
                HOME + to_core,
                zs * 2 + to_core,
                y_from,
                HOME + core,
            )

    def weight_in(n):
        rows = pl.ds(n * TILE, TILE)
        gin[rows, :] = lax.dot_general(
            xg[0, :, :, :, :, rows].reshape(NZ * NY * 2 * SLOTS, TILE),
            hp[1].reshape(NZ * NY * 2 * SLOTS, F_LOC),
            (((0,), (0,)), ((), ())),
            preferred_element_type=F32,
        ).astype(BF16)
        store(gin, gin_ref, rows, n)

    def weight_out(n):
        if n == 0:
            for k in range(NZ - 1):
                gathered(k, 0)
        rows = pl.ds(n * TILE, TILE)
        acc[rows, :] = lax.dot_general(
            hp[0, : NZ - 1, :, :, :, rows].reshape((NZ - 1) * NY * 2 * SLOTS, TILE),
            xg[1, : NZ - 1].reshape((NZ - 1) * NY * 2 * SLOTS, D_LOC),
            (((0,), (0,)), ((), ())),
            preferred_element_type=F32,
        )

    def weight_out_last(n):
        if n == 0:
            gathered(NZ - 1, 0)
        rows = pl.ds(n * TILE, TILE)
        part = lax.dot_general(
            hp[0, NZ - 1, :, :, :, rows].reshape(NY * 2 * SLOTS, TILE),
            xg[1, NZ - 1].reshape(NY * 2 * SLOTS, D_LOC),
            (((0,), (0,)), ((), ())),
            preferred_element_type=F32,
        )
        gout[rows, :] = (acc[rows, :] + part).astype(BF16)
        store(gout, gout_ref, rows, 3 + n)

    def out_piece(dx, half):
        start = around(y - x - dx) * D_LOC + half * HALF
        return ing.at[:, pl.ds(pl.multiple_of(start, 128), HALF)]

    def out_copy(ref, j, dev):
        return pltpu.make_async_remote_copy(
            src_ref=ref,
            dst_ref=ref,
            send_sem=osend.at[j],
            recv_sem=orecv.at[j],
            device_id=dev,
            device_id_type=MESH,
        )

    def out_push(ref, j, dev):
        copy = out_copy(ref, j, dev)
        copy.start()
        sent.append(copy)

    def out_arrived(ref, j):
        out_copy(ref, j, z_dev).wait_recv()

    def combine():
        for k in range(NZ):
            for b in range(2):
                arrived(ret.at[around(zh - FROM_Z[k]) * 2 + b], k, HOME + b)
        contrib = jnp.dot(
            comb[...], ret[...].reshape(2 * NZ * SLOTS, HALF), preferred_element_type=F32
        )
        start = y_to * D_LOC + c * HALF
        ing[:, pl.ds(pl.multiple_of(start, 128), HALF)] = (
            us[...].astype(F32) + contrib
        ).astype(BF16)
        out_push(out_piece(0, c), O_Z, z_dev)
        for i in range(2):
            out_push(out_piece(0, c), O_OWN + i, x_dev[i])

    def out_other():
        out_arrived(out_piece(0, 1 - c), O_Z)
        for i in range(2):
            out_push(out_piece(0, 1 - c), O_OTHER + i, x_dev[i])

    def out_far():
        out_arrived(out_piece(-1, c), O_OWN)
        out_push(out_piece(-1, c), O_FWD, x_dev[0])
        out_arrived(out_piece(1, 1 - c), O_OTHER + 1)
        out_push(out_piece(1, 1 - c), O_FWD + 1, x_dev[1])

    def out_end():
        out_arrived(out_piece(1, c), O_OWN + 1)
        out_arrived(out_piece(-1, 1 - c), O_OTHER)
        out_arrived(out_piece(2, c), O_FWD)
        out_arrived(out_piece(2, 1 - c), O_FWD + 1)

    steps = dict(
        a=share_own,
        b=share_other,
        c=share_far,
        d=project,
        e=pass_sums,
        f=activate,
        o=lambda k: gather_own(k, 0),
        g=lambda k: gather_far(k, 1),
        q=lambda k: gather_far(k, 0),
        h=go_back,
        i=back_sums,
        j=back_across,
        l=send_home,
        u=weight_in,
        v=weight_out,
        x=weight_out_last,
        s=start_dispatch,
        w=lambda n: (combine, out_other, out_far, out_end)[n](),
    )
    for word in PLAN:
        steps[word[0]](*(int(n) for n in word[1:]))
    store(ing, ing_ref, pl.ds(0, ing.shape[0]), 7)
    for copy in stores:
        copy.wait()
    for copy in sent:
        copy.wait_send()


def on_device(layer_inputs, out_grad, routes, gates, w_in, w_out):
    tokens = layer_inputs.shape[0]
    vmem = pl.BlockSpec(memory_space=pltpu.VMEM)
    hbm = pl.BlockSpec(memory_space=pl.ANY)
    rows = NY * 2 * SLOTS
    flops = 5 * 2 * NZ * rows * D_LOC * F_LOC
    in_grads, grad_in, grad_out = pl.pallas_call(
        kernel,
        out_shape=(
            jax.ShapeDtypeStruct(layer_inputs.shape, BF16),
            jax.ShapeDtypeStruct((D_LOC, F_LOC), BF16),
            jax.ShapeDtypeStruct((F_LOC, D_LOC), BF16),
        ),
        in_specs=[hbm] * 2 + [vmem] * 2 + [hbm] * 2,
        out_specs=(hbm,) * 3,
        scratch_shapes=[
            pltpu.VMEM((2, NZ, NY, 2, SLOTS, D_LOC), BF16),
            pltpu.VMEM((NZ, 2, NY, 2, SLOTS, F_LOC), BF16),
            pltpu.VMEM((NZ, 2, 2, SLOTS, F_LOC), BF16),
            pltpu.VMEM((NZ, 2, 2, 2, SLOTS, F_LOC), BF16),
            pltpu.VMEM((2, NZ, NY, 2, SLOTS, F_LOC), BF16),
            pltpu.VMEM((NZ, NY, 2, SLOTS, D_LOC), BF16),
            pltpu.VMEM((NZ, 2, SLOTS, D_LOC), BF16),
            pltpu.VMEM((NZ, 2, 2, SLOTS, D_LOC), BF16),
            pltpu.VMEM((NZ, 2, SLOTS, HALF), BF16),
            pltpu.VMEM((NZ, 2, SLOTS, HALF), BF16),
            pltpu.VMEM((2 * NZ, SLOTS, HALF), BF16),
            pltpu.SemaphoreType.DMA((NZ, COPIES)),
            pltpu.SemaphoreType.DMA((NZ, COPIES)),
            pltpu.SemaphoreType.DMA((OUT_COPIES,)),
            pltpu.SemaphoreType.DMA((OUT_COPIES,)),
            pltpu.SemaphoreType.DMA((12,)),
            pltpu.VMEM((D_LOC, F_LOC), BF16),
            pltpu.VMEM((F_LOC, D_LOC), BF16),
            pltpu.VMEM((D_LOC, F_LOC), BF16),
            pltpu.VMEM((F_LOC, D_LOC), BF16),
            pltpu.VMEM(layer_inputs.shape, BF16),
            pltpu.VMEM((F_LOC, D_LOC), F32),
            pltpu.VMEM((tokens, HALF), BF16),
            pltpu.VMEM((tokens, HALF), BF16),
            pltpu.VMEM((2, 2 * NZ, SLOTS, HALF), BF16),
            pltpu.VMEM((tokens, 2 * NZ * SLOTS), BF16),
        ],
        compiler_params=pltpu.CompilerParams(
            collective_id=0, has_side_effects=True, vmem_limit_bytes=56 * 2**20
        ),
        cost_estimate=pl.CostEstimate(flops=flops, bytes_accessed=2**23, transcendentals=0),
    )(layer_inputs, out_grad, routes, gates, w_in[0], w_out[0])
    return (in_grads, grad_in[None], grad_out[None])


def solution(mesh):
    assert dict(mesh.shape) == {"section": 2 * NX, "expert": 2 * NZ, "dp": NY}
    return jax.shard_map(
        on_device,
        mesh=mesh,
        in_specs=(
            P(("expert", "dp"), None),
            P(("expert", "dp"), None),
            P(("expert", "dp"), None),
            P(("expert", "dp"), None),
            P("expert", "dp", "section"),
            P("expert", "section", "dp"),
        ),
        out_specs=(
            P(("expert", "dp"), None),
            P("expert", "dp", "section"),
            P("expert", "section", "dp"),
        ),
        check_vma=False,
    )
```

time: 412 us -> 167 us (0.41)
  waiting for transfers between devices: 258 us -> 0 us
  Pallas kernels: 0 us -> 157 us
  matrix products: 52.5 us -> 0 us
  starting transfers between devices: 47.6 us -> 0 us
  blocking collectives: 36.1 us -> 0 us
  between operations: 14 us -> 0.65 us
  local copies, waits for them, and re-layouts: 1.27 us -> 8.13 us
    pallas_call x0 -> x1, Pallas kernels: none -> 157 us  [on_device(): pl.pallas_call(kernel, out_shape=(jax.ShapeDtypeStruct(layer_inputs.shape...]
    all_to_all x5 -> x0, waiting for transfers between devices: 103 us -> none  [the longest x2 49.4 us: on_device(): lax.all_to_all(send_rows.reshape(expert_count, capacity, width), 'expert'...]
    psum x1 -> x0, waiting for transfers between devices: 70.7 us -> none  [on_device(): back = lax.psum(back_part.astype(jnp.bfloat16), 'section')]
    reduce_scatter x2 -> x0, waiting for transfers between devices: 65.5 us -> none  [the longest x1 65.5 us: on_device(): lax.psum_scatter(acc_in.astype(jnp.bfloat16), 'dp', scatter_dimension=0,...]
    dot_general x20 -> x0, matrix products: 52.5 us -> none  [the longest x4 20.8 us: right_dot(): lax.dot_general(left, right, (((1,), (1,)), ((), ())), preferred_element_...]
    all_to_all x5 -> x0, starting transfers between devices: 47.3 us -> none  [the longest x2 18.7 us: on_device(): lax.all_to_all(send_rows.reshape(expert_count, capacity, width), 'expert'...]
    all_to_all x1 -> x0, blocking collectives: 36.1 us -> none  [send_home(): lax.all_to_all(back.reshape(expert_count, capacity, width), 'expert', spl...]
    all_gather x2 -> x0, waiting for transfers between devices: 18 us -> none  [the longest x1 18 us: on_device(): lax.all_gather(w_out_local, 'dp', axis=1, tiled=True)]
  transfers between devices with their start and end apart: 10 -> 0, of which waited for: 7 -> 0; matrix products, arithmetic and copies ran while one was open for 11% -> 0% of each run, Pallas kernels for 0% -> 0%
where the time goes in v1:
time: 167 us; the launch traced here: 165 us
  Pallas kernels  157 us (94%)
  local copies, waits for them, and re-layouts  8.13 us (5%)
    pallas_call x1, Pallas kernels, on_device(): pl.pallas_call(kernel, out_shape=(jax.ShapeDtypeStruct(layer_inputs.shape...  157 us
    unnamed x9, local copies, waits for them, and re-layouts  8.13 us

profile of v1, /device:TPU:1, one launch (start us, length us, event | category | flops | bytes accessed | tf_op | source)
XLA Modules:
  0.0 165.3 jit_solution(14988155472667876241)
XLA Ops:
  0.6 1.4 copy.9.routes_ref
  2.0 1.4 copy.10.gates_ref
  3.5 156.5 %shard_map.85 = (bf16[128,3072]{1,0:T(8,128)(2,1)}, bf16[768,1024]{1,0:T(8,128)(2,1)}, bf16[1024,768]{1,0:T(8,128)(2,1)}) custom-call(bf16[128,3072]{1,0:T(8,128)(2,1)} %x_ref.1, bf16[128,3072]{1,0:T(8,128)(2,1)} %up_ref.1, s32[128,2]{1,0:T(8,128)} %copy.9.routes_ref, f32[128,2]{1,0:T(8,128)} %copy.10.gates_ref, bf16[768,1024]{1,0:T(8,128)(2,1)} %bitcast.6, ...), custom_call_target="tpu_custom_call" | custom-call | flops 12079595520 | bytes 8388608 | tf_op jit(solution)/shard_map/pallas_call | solution.py:498
  160.0 0.0 copy-start.1
  160.0 2.2 %copy.14 = bf16[128,3072]{1,0:T(8,128)(2,1)} copy(bf16[128,3072]{1,0:T(8,128)(2,1)} %get-tuple-element.12) | data formatting | bytes 1572864
  162.2 0.0 copy-done.1
  162.2 0.0 copy-start
  162.2 1.1 copy.15
  163.3 0.8 copy-done
  164.1 1.1 copy.16
Async XLA Ops:
  160.0 2.2 %copy-start.1 = (bf16[768,1024]{1,0:T(8,128)(2,1)S(1)}, bf16[768,1024]{1,0:T(8,128)(2,1)}, u32[]{:S(2)}) copy-start(bf16[768,1024]{1,0:T(8,128)(2,1)} %get-tuple-element.7) | copy-start | bytes 4718596
  162.2 2.0 %copy-start = (bf16[1024,768]{1,0:T(8,128)(2,1)S(1)}, bf16[1024,768]{1,0:T(8,128)(2,1)}, u32[]{:S(2)}) copy-start(bf16[1024,768]{1,0:T(8,128)(2,1)} %get-tuple-element.8) | copy-start | bytes 4718596

commit v2 on v1

--- a/solution.py
+++ b/solution.py
@@ -30,13 +30,14 @@
 O_Z, O_OWN, O_OTHER, O_FWD = 0, 1, 3, 5
 OUT_COPIES = 7
 PLAN = (
-    "s00", "s01", "a00", "b00", "s10", "c00", "a01", "b01", "s11", "d00", "c01", "a10", "b10", "s20",
-    "s21", "e00", "d01", "c10", "a11", "b11", "e01", "d10", "c11", "s30", "s31", "a20", "b20", "f0",
-    "e10", "d11", "c20", "a21", "b21", "g0", "e11", "d20", "c21", "a30", "b30", "f1", "e20", "d21",
-    "c30", "a31", "b31", "g1", "h0", "e21", "d30", "c31", "f2", "e30", "d31", "g2", "h1", "i0",
-    "e31", "f3", "i1", "j0", "h2", "g3", "o0", "o1", "o2", "o3", "j1", "l0", "i2", "h3",
-    "l1", "j2", "u0", "i3", "l2", "u1", "j3", "u2", "l3", "q0", "w0", "q1", "w1", "q2",
-    "w2", "q3", "v0", "v1", "v2", "v3", "x0", "x1", "x2", "x3", "w3",
+    "s01", "s00", "s10", "s31", "a01", "s20", "s11", "s30", "a00", "C01", "c01", "a20", "C00", "c00",
+    "s21", "d01", "a31", "b20", "d00", "a21", "c20", "b31", "e01", "C20", "b21", "a30", "C31", "e00",
+    "c31", "d20", "a10", "c21", "C21", "b30", "a11", "d31", "b11", "d21", "c10", "C30", "b10", "e31",
+    "C10", "e20", "C11", "c11", "e21", "d10", "d11", "e10", "c30", "d30", "f2", "e11", "e30", "g2",
+    "f1", "f3", "g1", "h2", "f0", "g3", "i2", "h1", "g0", "i1", "o0", "o2", "j2", "h3",
+    "j1", "h0", "u2", "l1", "i3", "i0", "o1", "u1", "j3", "l2", "q2", "j0", "u0", "l3",
+    "l0", "q1", "o3", "w0", "q0", "w1", "q3", "w2", "v2", "v3", "v0", "x0", "v1", "x1",
+    "x2", "x3", "w3",
 )
 
 
@@ -47,9 +48,9 @@
     gates_ref,
     w_in_ref,
     w_out_ref,
-    ing_ref,
-    gin_ref,
-    gout_ref,
+    ing,
+    gin,
+    gout,
     xg,
     ps,
     r1,
@@ -68,14 +69,12 @@
     lsem,
     w_in,
     w_out,
-    gin,
-    gout,
-    ing,
     acc,
     xs,
     us,
     send,
     comb,
+    gate,
 ):
     section = lax.axis_index("section")
     expert = lax.axis_index("expert")
@@ -94,7 +93,6 @@
     y_dev = ({"dp": around(y + 1)}, {"dp": around(y - 1)})
     y_to = around(y - x)
     y_from = around(y + x)
-    to_cols = pl.ds(pl.multiple_of(y_to * D_LOC + c * HALF, 128), HALF)
     mine = pl.ds(pl.multiple_of(c * HALF, 128), HALF)
     other = pl.ds(pl.multiple_of((1 - c) * HALF, 128), HALF)
 
@@ -102,70 +100,90 @@
         src, dst = (
             (w_in_ref, w_in),
             (w_out_ref, w_out),
-            (x_ref.at[:, to_cols], xs),
-            (up_ref.at[:, to_cols], us),
+            (x_ref, xs),
+            (up_ref, us),
         )[n]
         return pltpu.make_async_copy(src, dst, lsem.at[n])
 
     for n in (2, 3, 0, 1):
         load(n).start()
-    stores = []
-
-    def store(src, dst, rows, n):
-        copy = pltpu.make_async_copy(src.at[rows], dst.at[rows], lsem.at[4 + n])
-        copy.start()
-        stores.append(copy)
-
     barrier = pltpu.get_barrier_semaphore()
     for dev in x_dev + y_dev + (z_dev,):
         pl.semaphore_signal(barrier, inc=1, device_id=dev, device_id_type=MESH)
-    for e in range(2 * NZ):
-        for yy in (y_to, y_from):
-
-            @pl.when(jnp.logical_or(x != 0, expert != e))
-            def _(e=e, yy=yy):
-                pl.semaphore_signal(
-                    barrier,
-                    inc=1,
-                    device_id={"expert": jnp.int32(e), "dp": yy},
-                    device_id_type=MESH,
-                )
+    for k in range(NZ):
+        ahead, behind = around(zh + FROM_Z[k]), around(zh - FROM_Z[k])
+        pairs = [(behind, around(y - x - k)), (ahead, around(y + x + k))]
+        if k > 0:
+            pairs += [(ahead, y_from), (behind, y_to)]
+        for to_core in range(2):
+            for zz, yy in pairs:
+
+                def greet(e=zz * 2 + to_core, yy=yy):
+                    pl.semaphore_signal(
+                        barrier,
+                        inc=1,
+                        device_id={"expert": e, "dp": yy},
+                        device_id_type=MESH,
+                    )
+
+                if k > 0:
+                    greet()
+                else:
+                    pl.when(jnp.logical_or(x != 0, core != to_core))(greet)
 
     tokens, count = us.shape[0], 2 * NZ * SLOTS
-    place = lax.broadcasted_iota(jnp.int32, (tokens, count), 1)
-    expert_of = sum((place >= SLOTS * e).astype(jnp.int32) for e in range(1, 2 * NZ))
-    token = lax.broadcasted_iota(jnp.int32, (tokens, count), 0)
-    micro_start = jnp.where(token >= ROWS, SLOTS // 2, 0)
-    is_first = routes_ref[:, 0:1] == expert_of
-    is_second = routes_ref[:, 1:2] == expert_of
+    place = lax.broadcasted_iota(jnp.int32, (count, tokens), 0)
+    expert_of, slot = jnp.zeros_like(place), place
+    for k in range(NZ):
+        for b in range(2):
+            start = (2 * k + b) * SLOTS
+            here = place >= start
+            expert_of = jnp.where(here, around(zh - FROM_Z[k]) * 2 + b, expert_of)
+            slot = jnp.where(here, place - start, slot)
+    token = lax.broadcasted_iota(jnp.int32, (count, tokens), 1)
+    slot = slot - jnp.where(token >= ROWS, SLOTS // 2, 0)
+    is_first = routes_ref[0:1, :] == expert_of
+    is_second = routes_ref[1:2, :] == expert_of
     named = jnp.logical_or(is_first, is_second)
     row = lax.broadcasted_iota(jnp.int32, (tokens, tokens), 0)
     col = lax.broadcasted_iota(jnp.int32, (tokens, tokens), 1)
-    earlier = jnp.logical_and(col < row, col >= jnp.where(row >= ROWS, ROWS, 0))
+    earlier = jnp.logical_and(row < col, row >= jnp.where(col >= ROWS, ROWS, 0))
 
     def ones(mask):
         return jnp.where(mask, 1.0, 0.0).astype(BF16)
 
-    before = jnp.dot(ones(earlier), ones(named), preferred_element_type=F32)
-    slot = (place - SLOTS * expert_of - micro_start).astype(F32)
-    taken = jnp.logical_and(named, before == slot)
-    comb[...] = ones(taken)
-
-    def picked(mask, rows):
-        return lax.dot_general(
-            ones(mask), rows, (((0,), (0,)), ((), ())), preferred_element_type=F32
-        )
-
+    before = jnp.dot(ones(named), ones(earlier), preferred_element_type=F32)
+    taken = jnp.logical_and(named, before == slot.astype(F32))
+    comb[0] = ones(taken)
+    comb[1] = ones(jnp.logical_and(taken, is_first))
+    comb[2] = ones(jnp.logical_and(taken, is_second))
+    for i in range(2):
+        gate[i] = jnp.broadcast_to(gates_ref[i : i + 1, :], (tokens, tokens)).T
     load(2).wait()
-    send[0] = picked(taken, xs[...]).astype(BF16).reshape(2 * NZ, SLOTS, HALF)
     load(3).wait()
-    wide = us[...].astype(F32)
-    send[1] = (
-        picked(jnp.logical_and(taken, is_first), (gates_ref[:, 0:1] * wide).astype(BF16))
-        + picked(jnp.logical_and(taken, is_second), (gates_ref[:, 1:2] * wide).astype(BF16))
-    ).astype(BF16).reshape(2 * NZ, SLOTS, HALF)
-
-    pl.semaphore_wait(barrier, jnp.where(x == 0, 19, 21))
+
+    def pick(k, m):
+        rows = pl.ds(2 * k * SLOTS, 2 * SLOTS)
+        first = around(y - x - k) * D_LOC
+        for half in (0, 1) if k == 0 else (c,):
+            cols = pl.ds(pl.multiple_of(first + half * HALF, 128), HALF)
+            if m == 0:
+                part = jnp.dot(comb[0, rows], xs[:, cols], preferred_element_type=F32)
+            else:
+                part = 0.0
+                wide = us[:, cols].astype(F32)
+                for i in range(2):
+                    weight = jnp.concatenate([gate[i]] * (HALF // tokens), axis=1)
+                    part = part + jnp.dot(
+                        comb[1 + i, rows],
+                        (weight * wide).astype(BF16),
+                        preferred_element_type=F32,
+                    )
+            place_in = pl.ds(half * HALF, HALF) if k == 0 else mine
+            send[m, k, :, :, place_in] = part.astype(BF16).reshape(2, SLOTS, HALF)
+
+    pick(0, 0)
+    pl.semaphore_wait(barrier, jnp.where(x == 0, 31, 33))
 
     sent = []
 
@@ -211,41 +229,54 @@
 
         sent.append(Guarded())
 
+    def width(k):
+        return pl.ds(0, D_LOC) if k == 0 else mine
+
     def start_dispatch(k, m):
+        if (k, m) != (0, 0):
+            pick(k, m)
         zd = around(zh - FROM_Z[k])
         for to_core in range(2):
             e = zd * 2 + to_core
             push_expert(
-                send.at[m, e],
-                xg.at[m, k, y, core, :, mine],
+                send.at[m, k, to_core, :, width(k)],
+                xg.at[m, k, y, core, :, width(k)],
                 k,
                 PART * m + A2A + to_core,
                 e,
-                y_to,
+                around(y - x - k),
                 PART * m + A2A + core,
             )
 
     def piece(k, m, dx, cols):
-        return xg.at[m, k, around(y + x + dx), :, :, cols]
+        return xg.at[m, k, around(y + x + dx + k), :, :, cols]
 
     def share(ref, k, j, dev):
         push(ref, ref, k, j, dev)
 
     def share_own(k, m):
         for b in range(2):
-            arrived(xg.at[m, k, y_from, b, :, mine], k, PART * m + A2A + b)
-        share(piece(k, m, 0, mine), k, PART * m + BZ, z_dev)
+            arrived(xg.at[m, k, around(y + x + k), b, :, width(k)], k, PART * m + A2A + b)
+        if k > 0:
+            share(piece(k, m, 0, mine), k, PART * m + BZ, z_dev)
         for i in range(2):
             share(piece(k, m, 0, mine), k, PART * m + B_OWN + i, x_dev[i])
+        if k == 0:
+            share_both(k, m)
+
+    def share_both(k, m):
+        for i in range(2):
+            share(piece(k, m, 0, other), k, PART * m + B_OTHER + i, x_dev[i])
 
     def share_other(k, m):
         arrived(piece(k, m, 0, other), k, PART * m + BZ)
-        for i in range(2):
-            share(piece(k, m, 0, other), k, PART * m + B_OTHER + i, x_dev[i])
-
-    def share_far(k, m):
+        share_both(k, m)
+
+    def pass_right(k, m):
         arrived(piece(k, m, -1, mine), k, PART * m + B_OWN)
         share(piece(k, m, -1, mine), k, PART * m + B_FWD, x_dev[0])
+
+    def pass_left(k, m):
         arrived(piece(k, m, 1, other), k, PART * m + B_OTHER + 1)
         share(piece(k, m, 1, other), k, PART * m + B_FWD + 1, x_dev[1])
 
@@ -312,7 +343,12 @@
             arrived(hp.at[m, k, near], k, PART * m + G_OWN + i)
             share(hp.at[m, k, near, i], k, PART * m + G_FWD + i, y_dev[i])
 
+    seen = set()
+
     def gathered(k, m):
+        if (k, m) in seen:
+            return
+        seen.add((k, m))
         for i in range(2):
             arrived(hp.at[m, k, around(y + 2), i], k, PART * m + G_FWD + i)
 
@@ -363,7 +399,7 @@
         for to_core in range(2):
             push_expert(
                 rb.at[k, to_core],
-                ret.at[expert],
+                ret.at[2 * k + core],
                 k,
                 HOME + to_core,
                 zs * 2 + to_core,
@@ -372,6 +408,8 @@
             )
 
     def weight_in(n):
+        for k in range(NZ):
+            gathered(k, 1)
         rows = pl.ds(n * TILE, TILE)
         gin[rows, :] = lax.dot_general(
             xg[0, :, :, :, :, rows].reshape(NZ * NY * 2 * SLOTS, TILE),
@@ -379,12 +417,10 @@
             (((0,), (0,)), ((), ())),
             preferred_element_type=F32,
         ).astype(BF16)
-        store(gin, gin_ref, rows, n)
 
     def weight_out(n):
-        if n == 0:
-            for k in range(NZ - 1):
-                gathered(k, 0)
+        for k in range(NZ - 1):
+            gathered(k, 0)
         rows = pl.ds(n * TILE, TILE)
         acc[rows, :] = lax.dot_general(
             hp[0, : NZ - 1, :, :, :, rows].reshape((NZ - 1) * NY * 2 * SLOTS, TILE),
@@ -394,8 +430,7 @@
         )
 
     def weight_out_last(n):
-        if n == 0:
-            gathered(NZ - 1, 0)
+        gathered(NZ - 1, 0)
         rows = pl.ds(n * TILE, TILE)
         part = lax.dot_general(
             hp[0, NZ - 1, :, :, :, rows].reshape(NY * 2 * SLOTS, TILE),
@@ -404,7 +439,6 @@
             preferred_element_type=F32,
         )
         gout[rows, :] = (acc[rows, :] + part).astype(BF16)
-        store(gout, gout_ref, rows, 3 + n)
 
     def out_piece(dx, half):
         start = around(y - x - dx) * D_LOC + half * HALF
@@ -431,14 +465,16 @@
     def combine():
         for k in range(NZ):
             for b in range(2):
-                arrived(ret.at[around(zh - FROM_Z[k]) * 2 + b], k, HOME + b)
-        contrib = jnp.dot(
-            comb[...], ret[...].reshape(2 * NZ * SLOTS, HALF), preferred_element_type=F32
+                arrived(ret.at[2 * k + b], k, HOME + b)
+        contrib = lax.dot_general(
+            comb[0],
+            ret[...].reshape(2 * NZ * SLOTS, HALF),
+            (((0,), (0,)), ((), ())),
+            preferred_element_type=F32,
         )
         start = y_to * D_LOC + c * HALF
-        ing[:, pl.ds(pl.multiple_of(start, 128), HALF)] = (
-            us[...].astype(F32) + contrib
-        ).astype(BF16)
+        cols = pl.ds(pl.multiple_of(start, 128), HALF)
+        ing[:, cols] = (us[:, cols].astype(F32) + contrib).astype(BF16)
         out_push(out_piece(0, c), O_Z, z_dev)
         for i in range(2):
             out_push(out_piece(0, c), O_OWN + i, x_dev[i])
@@ -463,7 +499,8 @@
     steps = dict(
         a=share_own,
         b=share_other,
-        c=share_far,
+        c=pass_right,
+        C=pass_left,
         d=project,
         e=pass_sums,
         f=activate,
@@ -482,9 +519,6 @@
     )
     for word in PLAN:
         steps[word[0]](*(int(n) for n in word[1:]))
-    store(ing, ing_ref, pl.ds(0, ing.shape[0]), 7)
-    for copy in stores:
-        copy.wait()
     for copy in sent:
         copy.wait_send()
 
@@ -498,12 +532,12 @@
     in_grads, grad_in, grad_out = pl.pallas_call(
         kernel,
         out_shape=(
-            jax.ShapeDtypeStruct(layer_inputs.shape, BF16),
-            jax.ShapeDtypeStruct((D_LOC, F_LOC), BF16),
-            jax.ShapeDtypeStruct((F_LOC, D_LOC), BF16),
+            pltpu.VMEM(layer_inputs.shape, BF16),
+            pltpu.VMEM((D_LOC, F_LOC), BF16),
+            pltpu.VMEM((F_LOC, D_LOC), BF16),
         ),
         in_specs=[hbm] * 2 + [vmem] * 2 + [hbm] * 2,
-        out_specs=(hbm,) * 3,
+        out_specs=(vmem,) * 3,
         scratch_shapes=[
             pltpu.VMEM((2, NZ, NY, 2, SLOTS, D_LOC), BF16),
             pltpu.VMEM((NZ, 2, NY, 2, SLOTS, F_LOC), BF16),
@@ -520,23 +554,21 @@
             pltpu.SemaphoreType.DMA((NZ, COPIES)),
             pltpu.SemaphoreType.DMA((OUT_COPIES,)),
             pltpu.SemaphoreType.DMA((OUT_COPIES,)),
-            pltpu.SemaphoreType.DMA((12,)),
+            pltpu.SemaphoreType.DMA((4,)),
             pltpu.VMEM((D_LOC, F_LOC), BF16),
             pltpu.VMEM((F_LOC, D_LOC), BF16),
-            pltpu.VMEM((D_LOC, F_LOC), BF16),
-            pltpu.VMEM((F_LOC, D_LOC), BF16),
+            pltpu.VMEM((F_LOC, D_LOC), F32),
             pltpu.VMEM(layer_inputs.shape, BF16),
-            pltpu.VMEM((F_LOC, D_LOC), F32),
-            pltpu.VMEM((tokens, HALF), BF16),
-            pltpu.VMEM((tokens, HALF), BF16),
-            pltpu.VMEM((2, 2 * NZ, SLOTS, HALF), BF16),
-            pltpu.VMEM((tokens, 2 * NZ * SLOTS), BF16),
+            pltpu.VMEM(layer_inputs.shape, BF16),
+            pltpu.VMEM((2, NZ, 2, SLOTS, D_LOC), BF16),
+            pltpu.VMEM((3, 2 * NZ * SLOTS, tokens), BF16),
+            pltpu.VMEM((2, tokens, tokens), F32),
         ],
         compiler_params=pltpu.CompilerParams(
             collective_id=0, has_side_effects=True, vmem_limit_bytes=56 * 2**20
         ),
         cost_estimate=pl.CostEstimate(flops=flops, bytes_accessed=2**23, transcendentals=0),
-    )(layer_inputs, out_grad, routes, gates, w_in[0], w_out[0])
+    )(layer_inputs, out_grad, routes.T, gates.T, w_in[0], w_out[0])
     return (in_grads, grad_in[None], grad_out[None])
 
 

time: 167 us -> 151 us (0.904)
  Pallas kernels: 157 us -> 146 us
  local copies, waits for them, and re-layouts: 8.13 us -> 3.17 us
    pallas_call x1, Pallas kernels: 157 us -> 146 us  [on_device(): pl.pallas_call(kernel, out_shape=(pltpu.VMEM(layer_inputs.shape, BF16), p...]
    unnamed x9 -> x3, local copies, waits for them, and re-layouts: 8.13 us -> 3.17 us
where the time goes in v2:
time: 151 us; the launch traced here: 150 us
  Pallas kernels  146 us (97%)
  local copies, waits for them, and re-layouts  3.17 us (2%)
    pallas_call x1, Pallas kernels, on_device(): pl.pallas_call(kernel, out_shape=(pltpu.VMEM(layer_inputs.shape, BF16), p...  146 us
    unnamed x3, local copies, waits for them, and re-layouts  3.17 us

profile of v2, /device:TPU:1, one launch (start us, length us, event | category | flops | bytes accessed | tf_op | source)
XLA Modules:
  0.0 149.8 jit_solution(5906980582493474632)
XLA Ops:
  0.6 146.0 %shard_map.85 = (bf16[128,3072]{1,0:T(8,128)(2,1)S(1)}, bf16[768,1024]{1,0:T(8,128)(2,1)S(1)}, bf16[1024,768]{1,0:T(8,128)(2,1)S(1)}) custom-call(bf16[128,3072]{1,0:T(8,128)(2,1)} %x_ref.1, bf16[128,3072]{1,0:T(8,128)(2,1)} %up_ref.1, s32[2,128]{1,0:T(2,128)} %bitcast.10, f32[2,128]{1,0:T(2,128)} %bitcast.11, bf16[768,1024]{1,0:T(8,128)(2,1)} %bitcast.8, ...), custom_call_target="tpu_custom_call" | custom-call | flops 12079595520 | bytes 8388608 | tf_op jit(solution)/shard_map/pallas_call | solution.py:532
  146.6 0.9 copy.12
  147.5 1.1 copy.13
  148.7 1.1 copy.14

commit v3 on v2

--- a/solution.py
+++ b/solution.py
@@ -300,7 +300,7 @@
             ps[k, m, :, :, :, cols] = part.astype(BF16).reshape(NY, 2, SLOTS, TILE)
             return 0
 
-        lax.fori_loop(0, F_LOC // TILE, body, 0)
+        lax.fori_loop(0, F_LOC // TILE, body, 0, unroll=True)
         far, after, before = (around(y + d) for d in (2, 1, -1))
         j = PART * m
         push(ps.at[k, m, far, 0], r1.at[k, m, 0], k, j + R_FAR, y_dev[0])
@@ -366,7 +366,7 @@
             bk[k, :, :, :, cols] = part.astype(BF16).reshape(NY, 2, SLOTS, TILE)
             return 0
 
-        lax.fori_loop(0, D_LOC // TILE, body, 0)
+        lax.fori_loop(0, D_LOC // TILE, body, 0, unroll=True)
         far, after, before = (around(y + x + d) for d in (2, 1, -1))
         push(bk.at[k, far, 0], q1.at[k, 0], k, S_FAR, x_dev[0])
         push(bk.at[k, far, 1], q1.at[k, 1], k, S_FAR + 1, x_dev[1])
@@ -521,6 +521,35 @@
         steps[word[0]](*(int(n) for n in word[1:]))
     for copy in sent:
         copy.wait_send()
+
+
+def store_kernel(*refs):
+    *pairs, sem = refs
+    copies = []
+    for i in range(3):
+        src, dst = pairs[i], pairs[3 + i]
+        rows = src.shape[0] // 4
+        for n in range(4):
+            part = pl.ds(n * rows, rows)
+            copies.append(pltpu.make_async_copy(src.at[part], dst.at[part], sem.at[4 * i + n]))
+    for copy in copies:
+        copy.start()
+    for copy in copies:
+        copy.wait()
+
+
+def store_results(*arrays):
+    hbm = pl.BlockSpec(memory_space=pl.ANY)
+    size = sum(a.size * a.dtype.itemsize for a in arrays)
+    return pl.pallas_call(
+        store_kernel,
+        out_shape=tuple(jax.ShapeDtypeStruct(a.shape, a.dtype) for a in arrays),
+        in_specs=[hbm] * 3,
+        out_specs=(hbm,) * 3,
+        scratch_shapes=[pltpu.SemaphoreType.DMA((12,))],
+        compiler_params=pltpu.CompilerParams(vmem_limit_bytes=2**20),
+        cost_estimate=pl.CostEstimate(flops=0, bytes_accessed=size, transcendentals=0),
+    )(*(pltpu.with_memory_space_constraint(a, pltpu.VMEM) for a in arrays))
 
 
 def on_device(layer_inputs, out_grad, routes, gates, w_in, w_out):
@@ -565,10 +594,11 @@
             pltpu.VMEM((2, tokens, tokens), F32),
         ],
         compiler_params=pltpu.CompilerParams(
-            collective_id=0, has_side_effects=True, vmem_limit_bytes=56 * 2**20
+            collective_id=0, has_side_effects=True, vmem_limit_bytes=50 * 2**20
         ),
         cost_estimate=pl.CostEstimate(flops=flops, bytes_accessed=2**23, transcendentals=0),
     )(layer_inputs, out_grad, routes.T, gates.T, w_in[0], w_out[0])
+    in_grads, grad_in, grad_out = store_results(in_grads, grad_in, grad_out)
     return (in_grads, grad_in[None], grad_out[None])
 
 

time: 151 us -> 150 us (level)
  local copies, waits for them, and re-layouts: 3.17 us -> 1.35 us
    pallas_call x0 -> x1, Pallas kernels: none -> 2.02 us  [store_results(): pl.pallas_call(store_kernel, out_shape=tuple((jax.ShapeDtypeStruct(a.shap...]
    unnamed x3 -> x4, local copies, waits for them, and re-layouts: 3.17 us -> 1.35 us
where the time goes in v3:
time: 150 us; the launch traced here: 149 us
  Pallas kernels  147 us (98%)
    pallas_call x1, Pallas kernels, on_device(): pl.pallas_call(kernel, out_shape=(pltpu.VMEM(layer_inputs.shape, BF16), p...  145 us

profile of v3, /device:TPU:1, one launch (start us, length us, event | category | flops | bytes accessed | tf_op | source)
XLA Modules:
  0.0 148.9 jit_solution(764072198574695762)
XLA Ops:
  0.6 0.0 copy-start
  0.6 0.7 copy-done
  1.3 0.0 copy-start.1
  1.3 0.7 copy-done.1
  2.0 144.8 %shard_map.85 = (bf16[128,3072]{1,0:T(8,128)(2,1)S(1)}, bf16[768,1024]{1,0:T(8,128)(2,1)S(1)}, bf16[1024,768]{1,0:T(8,128)(2,1)S(1)}) custom-call(bf16[128,3072]{1,0:T(8,128)(2,1)} %x_ref.1, bf16[128,3072]{1,0:T(8,128)(2,1)} %up_ref.1, s32[2,128]{1,0:T(2,128)S(1)} %bitcast.6, f32[2,128]{1,0:T(2,128)S(1)} %bitcast.7, bf16[768,1024]{1,0:T(8,128)(2,1)} %bitcast.8, ...), custom_call_target="tpu_custom_call" | custom-call | flops 12079595520 | bytes 8388608 | tf_op jit(solution)/shard_map/pallas_call | solution.py:561
  146.8 2.0 %shard_map.86 = (bf16[128,3072]{1,0:T(8,128)(2,1)}, bf16[768,1024]{1,0:T(8,128)(2,1)}, bf16[1024,768]{1,0:T(8,128)(2,1)}) custom-call(bf16[128,3072]{1,0:T(8,128)(2,1)S(1)} %get-tuple-element.9.refs_0_, bf16[768,1024]{1,0:T(8,128)(2,1)S(1)} %get-tuple-element.10.refs_1_, bf16[1024,768]{1,0:T(8,128)(2,1)S(1)} %get-tuple-element.11.refs_2_), custom_call_target="tpu_custom_call" | custom-call | bytes 3932160 | tf_op jit(solution)/shard_map/pallas_call | solution.py:544
Async XLA Ops:
  0.6 0.7 copy-start
  1.3 0.7 copy-start.1

commit v4 on v3

--- a/solution.py
+++ b/solution.py
@@ -24,20 +24,25 @@
 R_FAR, R_NEAR, R_SUM = 9, 11, 13
 G_OWN, G_FWD = 15, 17
 PART = 19
-S_FAR, S_NEAR, S_SUM, S_Z = 38, 40, 42, 44
-HOME = 45
-COPIES = 47
-O_Z, O_OWN, O_OTHER, O_FWD = 0, 1, 3, 5
-OUT_COPIES = 7
+S_FAR, S_NEAR, S_SUM = 38, 40, 42
+S_PART = 6
+S_Z = 50
+HOME = 51
+COPIES = 53
+O_Z, O_OWN, O_OTHER, O_FWD = 0, 2, 4, 8
+OUT_COPIES = 12
 PLAN = (
-    "s01", "s00", "s10", "s31", "a01", "s20", "s11", "s30", "a00", "C01", "c01", "a20", "C00", "c00",
-    "s21", "d01", "a31", "b20", "d00", "a21", "c20", "b31", "e01", "C20", "b21", "a30", "C31", "e00",
-    "c31", "d20", "a10", "c21", "C21", "b30", "a11", "d31", "b11", "d21", "c10", "C30", "b10", "e31",
-    "C10", "e20", "C11", "c11", "e21", "d10", "d11", "e10", "c30", "d30", "f2", "e11", "e30", "g2",
-    "f1", "f3", "g1", "h2", "f0", "g3", "i2", "h1", "g0", "i1", "o0", "o2", "j2", "h3",
-    "j1", "h0", "u2", "l1", "i3", "i0", "o1", "u1", "j3", "l2", "q2", "j0", "u0", "l3",
-    "l0", "q1", "o3", "w0", "q0", "w1", "q3", "w2", "v2", "v3", "v0", "x0", "v1", "x1",
-    "x2", "x3", "w3",
+    "s00", "s20", "s01", "s11", "s30", "a001", "a000", "a011", "s21", "c001", "C001", "a20",
+    "s31", "c000", "s10", "C000", "C011", "c011", "d001", "a010", "b20", "a21", "d000", "d011",
+    "C010", "c010", "c20", "C20", "e001", "e000", "d010", "b21", "c21", "a11", "d20", "C21",
+    "b11", "a10", "e011", "a31", "e010", "d21", "C11", "b10", "e200", "e201", "c11", "a30",
+    "e211", "e210", "b30", "b31", "d11", "C10", "c30", "f2", "c31", "c10", "C31", "e111",
+    "d10", "d31", "e100", "g2", "e110", "e101", "C30", "d30", "e311", "e300", "e301", "h2",
+    "e310", "f1", "f3", "i21", "g1", "i20", "f0", "g3", "h1", "o1", "j2", "i10",
+    "h3", "g0", "i30", "o0", "j1", "o2", "i11", "h0", "l1", "u1", "j3", "i00",
+    "l2", "i01", "i31", "q0", "j0", "u0", "l3", "l0", "o3", "w0", "q2", "q1",
+    "w10", "q3", "w11", "u2", "w30", "w2", "w31", "v2", "v1", "v0", "v3", "x0",
+    "x3", "x1", "x2", "w4",
 )
 
 
@@ -96,6 +101,9 @@
     mine = pl.ds(pl.multiple_of(c * HALF, 128), HALF)
     other = pl.ds(pl.multiple_of((1 - c) * HALF, 128), HALF)
 
+    def shift(k):
+        return x + k + 2
+
     def load(n):
         src, dst = (
             (w_in_ref, w_in),
@@ -112,11 +120,14 @@
         pl.semaphore_signal(barrier, inc=1, device_id=dev, device_id_type=MESH)
     for k in range(NZ):
         ahead, behind = around(zh + FROM_Z[k]), around(zh - FROM_Z[k])
-        pairs = [(behind, around(y - x - k)), (ahead, around(y + x + k))]
-        if k > 0:
-            pairs += [(ahead, y_from), (behind, y_to)]
+        pairs = [
+            (behind, around(y - shift(k)), k > 0 or around(shift(k)) != 0),
+            (ahead, around(y + shift(k)), k > 0 or around(shift(k)) != 0),
+            (ahead, y_from, k > 0 or x != 0),
+            (behind, y_to, k > 0 or x != 0),
+        ]
         for to_core in range(2):
-            for zz, yy in pairs:
+            for zz, yy, away in pairs:
 
                 def greet(e=zz * 2 + to_core, yy=yy):
                     pl.semaphore_signal(
@@ -129,7 +140,7 @@
                 if k > 0:
                     greet()
                 else:
-                    pl.when(jnp.logical_or(x != 0, core != to_core))(greet)
+                    pl.when(jnp.logical_or(away, core != to_core))(greet)
 
     tokens, count = us.shape[0], 2 * NZ * SLOTS
     place = lax.broadcasted_iota(jnp.int32, (count, tokens), 0)
@@ -155,16 +166,19 @@
     before = jnp.dot(ones(named), ones(earlier), preferred_element_type=F32)
     taken = jnp.logical_and(named, before == slot.astype(F32))
     comb[0] = ones(taken)
-    comb[1] = ones(jnp.logical_and(taken, is_first))
-    comb[2] = ones(jnp.logical_and(taken, is_second))
-    for i in range(2):
-        gate[i] = jnp.broadcast_to(gates_ref[i : i + 1, :], (tokens, tokens)).T
     load(2).wait()
-    load(3).wait()
+
+    prepared = []
+
+    def prepare_grads():
+        for i, mask in enumerate((is_first, is_second)):
+            comb[1 + i] = ones(jnp.logical_and(taken, mask))
+            gate[i] = jnp.broadcast_to(gates_ref[i : i + 1, :], (tokens, tokens)).T
+        load(3).wait()
 
     def pick(k, m):
         rows = pl.ds(2 * k * SLOTS, 2 * SLOTS)
-        first = around(y - x - k) * D_LOC
+        first = around(y - shift(k)) * D_LOC
         for half in (0, 1) if k == 0 else (c,):
             cols = pl.ds(pl.multiple_of(first + half * HALF, 128), HALF)
             if m == 0:
@@ -183,7 +197,7 @@
             send[m, k, :, :, place_in] = part.astype(BF16).reshape(2, SLOTS, HALF)
 
     pick(0, 0)
-    pl.semaphore_wait(barrier, jnp.where(x == 0, 31, 33))
+    pl.semaphore_wait(barrier, jnp.where(lax.rem(x, 2) == 0, 35, 37))
 
     sent = []
 
@@ -205,11 +219,11 @@
     def arrived(dst, k, j):
         remote(dst, dst, k, j, z_dev).wait_recv()
 
-    def push_expert(src, dst, k, j, e, yy, rj):
+    def push_expert(src, dst, k, j, e, yy, rj, level):
         if k != 0:
             push(src, dst, k, j, {"expert": e, "dp": yy}, rj)
             return
-        own = jnp.logical_and(x == 0, expert == e)
+        own = jnp.logical_and(level, expert == e)
         copy = remote(src, dst, k, j, {"expert": e, "dp": yy}, rj)
         local = pltpu.make_async_copy(src, dst, rsem.at[k, rj])
 
@@ -233,6 +247,9 @@
         return pl.ds(0, D_LOC) if k == 0 else mine
 
     def start_dispatch(k, m):
+        if m == 1 and not prepared:
+            prepared.append(True)
+            prepare_grads()
         if (k, m) != (0, 0):
             pick(k, m)
         zd = around(zh - FROM_Z[k])
@@ -244,77 +261,89 @@
                 k,
                 PART * m + A2A + to_core,
                 e,
-                around(y - x - k),
+                around(y - shift(k)),
                 PART * m + A2A + core,
+                around(shift(k)) == 0,
             )
 
-    def piece(k, m, dx, cols):
-        return xg.at[m, k, around(y + x + dx + k), :, :, cols]
+    def piece(k, m, dx, cols, b):
+        return xg.at[m, k, around(y + dx + shift(k)), slice(None) if b is None else b, :, cols]
+
+    def sems(k, b):
+        return NZ if b == 1 else k
 
     def share(ref, k, j, dev):
         push(ref, ref, k, j, dev)
 
-    def share_own(k, m):
-        for b in range(2):
-            arrived(xg.at[m, k, around(y + x + k), b, :, width(k)], k, PART * m + A2A + b)
+    def share_own(k, m, b=None):
+        for i in (0, 1) if b is None else (b,):
+            rows = xg.at[m, k, around(y + shift(k)), i, :, width(k)]
+            arrived(rows, k, PART * m + A2A + i)
         if k > 0:
-            share(piece(k, m, 0, mine), k, PART * m + BZ, z_dev)
-        for i in range(2):
-            share(piece(k, m, 0, mine), k, PART * m + B_OWN + i, x_dev[i])
+            share(piece(k, m, 0, mine, b), k, PART * m + BZ, z_dev)
+        for i in range(2):
+            share(piece(k, m, 0, mine, b), sems(k, b), PART * m + B_OWN + i, x_dev[i])
         if k == 0:
-            share_both(k, m)
-
-    def share_both(k, m):
-        for i in range(2):
-            share(piece(k, m, 0, other), k, PART * m + B_OTHER + i, x_dev[i])
+            share_both(k, m, b)
+
+    def share_both(k, m, b=None):
+        for i in range(2):
+            share(piece(k, m, 0, other, b), sems(k, b), PART * m + B_OTHER + i, x_dev[i])
 
     def share_other(k, m):
-        arrived(piece(k, m, 0, other), k, PART * m + BZ)
+        arrived(piece(k, m, 0, other, None), k, PART * m + BZ)
         share_both(k, m)
 
-    def pass_right(k, m):
-        arrived(piece(k, m, -1, mine), k, PART * m + B_OWN)
-        share(piece(k, m, -1, mine), k, PART * m + B_FWD, x_dev[0])
-
-    def pass_left(k, m):
-        arrived(piece(k, m, 1, other), k, PART * m + B_OTHER + 1)
-        share(piece(k, m, 1, other), k, PART * m + B_FWD + 1, x_dev[1])
-
-    def project(k, m):
-        if k == 0:
+    def pass_right(k, m, b=None):
+        arrived(piece(k, m, -1, mine, b), sems(k, b), PART * m + B_OWN)
+        share(piece(k, m, -1, mine, b), sems(k, b), PART * m + B_FWD, x_dev[0])
+
+    def pass_left(k, m, b=None):
+        arrived(piece(k, m, 1, other, b), sems(k, b), PART * m + B_OTHER + 1)
+        share(piece(k, m, 1, other, b), sems(k, b), PART * m + B_FWD + 1, x_dev[1])
+
+    loaded = set()
+
+    def project(k, m, b=None):
+        if m not in loaded:
+            loaded.add(m)
             load(m).wait()
-        arrived(piece(k, m, 1, mine), k, PART * m + B_OWN + 1)
-        arrived(piece(k, m, -1, other), k, PART * m + B_OTHER)
-        arrived(piece(k, m, 2, mine), k, PART * m + B_FWD)
-        arrived(piece(k, m, 2, other), k, PART * m + B_FWD + 1)
+        arrived(piece(k, m, 1, mine, b), sems(k, b), PART * m + B_OWN + 1)
+        arrived(piece(k, m, -1, other, b), sems(k, b), PART * m + B_OTHER)
+        arrived(piece(k, m, 2, mine, b), sems(k, b), PART * m + B_FWD)
+        arrived(piece(k, m, 2, other, b), sems(k, b), PART * m + B_FWD + 1)
+        which = slice(None) if b is None else slice(b, b + 1)
+        count = 2 if b is None else 1
 
         def body(n, _):
             cols = pl.ds(pl.multiple_of(n * TILE, TILE), TILE)
-            rows = xg[m, k].reshape(NY * 2 * SLOTS, D_LOC)
+            rows = xg[m, k, :, which].reshape(NY * count * SLOTS, D_LOC)
             if m == 0:
                 part = jnp.dot(rows, w_in[:, cols], preferred_element_type=F32)
             else:
                 part = lax.dot_general(
                     rows, w_out[cols, :], (((1,), (1,)), ((), ())), preferred_element_type=F32
                 )
-            ps[k, m, :, :, :, cols] = part.astype(BF16).reshape(NY, 2, SLOTS, TILE)
+            ps[k, m, :, which, :, cols] = part.astype(BF16).reshape(NY, count, SLOTS, TILE)
             return 0
 
         lax.fori_loop(0, F_LOC // TILE, body, 0, unroll=True)
         far, after, before = (around(y + d) for d in (2, 1, -1))
         j = PART * m
-        push(ps.at[k, m, far, 0], r1.at[k, m, 0], k, j + R_FAR, y_dev[0])
-        push(ps.at[k, m, far, 1], r1.at[k, m, 1], k, j + R_FAR + 1, y_dev[1])
-        push(ps.at[k, m, after, 1], r2.at[k, m, 0, 1], k, j + R_NEAR, y_dev[0])
-        push(ps.at[k, m, before, 0], r2.at[k, m, 1, 0], k, j + R_NEAR + 1, y_dev[1])
-
-    def pass_sums(k, m):
-        for i in range(2):
-            arrived(r1.at[k, m, i], k, PART * m + R_FAR + i)
-            to = around(y + 1 - 2 * i)
-            total = ps[k, m, to, i].astype(F32) + r1[k, m, i].astype(F32)
-            ps[k, m, to, i] = total.astype(BF16)
-            push(ps.at[k, m, to, i], r2.at[k, m, i, i], k, PART * m + R_SUM + i, y_dev[i])
+        if b != 1:
+            push(ps.at[k, m, far, 0], r1.at[k, m, 0], k, j + R_FAR, y_dev[0])
+        if b != 0:
+            push(ps.at[k, m, far, 1], r1.at[k, m, 1], k, j + R_FAR + 1, y_dev[1])
+            push(ps.at[k, m, after, 1], r2.at[k, m, 0, 1], k, j + R_NEAR, y_dev[0])
+        if b != 1:
+            push(ps.at[k, m, before, 0], r2.at[k, m, 1, 0], k, j + R_NEAR + 1, y_dev[1])
+
+    def pass_sums(k, m, i):
+        arrived(r1.at[k, m, i], k, PART * m + R_FAR + i)
+        to = around(y + 1 - 2 * i)
+        total = ps[k, m, to, i].astype(F32) + r1[k, m, i].astype(F32)
+        ps[k, m, to, i] = total.astype(BF16)
+        push(ps.at[k, m, to, i], r2.at[k, m, i, i], k, PART * m + R_SUM + i, y_dev[i])
 
     def activate(k):
         for m in range(2):
@@ -368,33 +397,42 @@
 
         lax.fori_loop(0, D_LOC // TILE, body, 0, unroll=True)
         far, after, before = (around(y + x + d) for d in (2, 1, -1))
-        push(bk.at[k, far, 0], q1.at[k, 0], k, S_FAR, x_dev[0])
-        push(bk.at[k, far, 1], q1.at[k, 1], k, S_FAR + 1, x_dev[1])
-        push(bk.at[k, after, 1], q2.at[k, 0, 1], k, S_NEAR, x_dev[0])
-        push(bk.at[k, before, 0], q2.at[k, 1, 0], k, S_NEAR + 1, x_dev[1])
-
-    def back_sums(k):
-        for i in range(2):
-            arrived(q1.at[k, i], k, S_FAR + i)
+        for h, cols in enumerate((other, mine)):
+            j = S_PART * h
+            push(bk.at[k, far, 0, :, cols], q1.at[k, 0, :, cols], k, j + S_FAR, x_dev[0])
+            push(bk.at[k, far, 1, :, cols], q1.at[k, 1, :, cols], k, j + S_FAR + 1, x_dev[1])
+            push(bk.at[k, after, 1, :, cols], q2.at[k, 0, 1, :, cols], k, j + S_NEAR, x_dev[0])
+            push(bk.at[k, before, 0, :, cols], q2.at[k, 1, 0, :, cols], k, j + S_NEAR + 1, x_dev[1])
+
+    def back_sums(k, h):
+        cols = (other, mine)[h]
+        j = S_PART * h
+        for i in range(2):
+            arrived(q1.at[k, i, :, cols], k, j + S_FAR + i)
             to = around(y + x + 1 - 2 * i)
-            total = bk[k, to, i].astype(F32) + q1[k, i].astype(F32)
-            bk[k, to, i] = total.astype(BF16)
-            push(bk.at[k, to, i], q2.at[k, i, i], k, S_SUM + i, x_dev[i])
+            total = bk[k, to, i, :, cols].astype(F32) + q1[k, i, :, cols].astype(F32)
+            bk[k, to, i, :, cols] = total.astype(BF16)
+            push(bk.at[k, to, i, :, cols], q2.at[k, i, i, :, cols], k, j + S_SUM + i, x_dev[i])
+
+    def back_total(k, h):
+        cols = (other, mine)[h]
+        j = S_PART * h
+        for i in range(2):
+            arrived(q2.at[k, i, 1 - i, :, cols], k, j + S_NEAR + i)
+            arrived(q2.at[k, i, i, :, cols], k, j + S_SUM + i)
+        return (
+            bk[k, y_from, :, :, cols].astype(F32)
+            + q2[k, 0, :, :, cols].astype(F32)
+            + q2[k, 1, :, :, cols].astype(F32)
+        )
 
     def back_across(k):
-        for i in range(2):
-            arrived(q2.at[k, i, 1 - i], k, S_NEAR + i)
-            arrived(q2.at[k, i, i], k, S_SUM + i)
-        for b in range(2):
-            total = (
-                bk[k, y_from, b].astype(F32) + q2[k, 0, b].astype(F32) + q2[k, 1, b].astype(F32)
-            )
-            bk[k, y_from, b] = total.astype(BF16)
+        bk[k, y_from, :, :, other] = back_total(k, 0).astype(BF16)
         push(bk.at[k, y_from, :, :, other], q3.at[k], k, S_Z, z_dev)
 
     def send_home(k):
         arrived(q3.at[k], k, S_Z)
-        rb[k] = (bk[k, y_from, :, :, mine].astype(F32) + q3[k].astype(F32)).astype(BF16)
+        rb[k] = (back_total(k, 1) + q3[k].astype(F32)).astype(BF16)
         zs = around(zh + FROM_Z[k])
         for to_core in range(2):
             push_expert(
@@ -405,6 +443,7 @@
                 zs * 2 + to_core,
                 y_from,
                 HOME + core,
+                x == 0,
             )
 
     def weight_in(n):
@@ -440,9 +479,10 @@
         )
         gout[rows, :] = (acc[rows, :] + part).astype(BF16)
 
-    def out_piece(dx, half):
+    def out_piece(dx, half, n=None):
         start = around(y - x - dx) * D_LOC + half * HALF
-        return ing.at[:, pl.ds(pl.multiple_of(start, 128), HALF)]
+        rows = pl.ds(0, ing.shape[0]) if n is None else pl.ds(n * ROWS, ROWS)
+        return ing.at[rows, pl.ds(pl.multiple_of(start, 128), HALF)]
 
     def out_copy(ref, j, dev):
         return pltpu.make_async_remote_copy(
@@ -475,26 +515,30 @@
         start = y_to * D_LOC + c * HALF
         cols = pl.ds(pl.multiple_of(start, 128), HALF)
         ing[:, cols] = (us[:, cols].astype(F32) + contrib).astype(BF16)
-        out_push(out_piece(0, c), O_Z, z_dev)
+        for n in range(2):
+            out_push(out_piece(0, c, n), O_Z + n, z_dev)
         for i in range(2):
             out_push(out_piece(0, c), O_OWN + i, x_dev[i])
 
-    def out_other():
-        out_arrived(out_piece(0, 1 - c), O_Z)
-        for i in range(2):
-            out_push(out_piece(0, 1 - c), O_OTHER + i, x_dev[i])
-
-    def out_far():
+    def out_other(n):
+        out_arrived(out_piece(0, 1 - c, n), O_Z + n)
+        for i in range(2):
+            out_push(out_piece(0, 1 - c, n), O_OTHER + 2 * n + i, x_dev[i])
+
+    def out_right():
         out_arrived(out_piece(-1, c), O_OWN)
         out_push(out_piece(-1, c), O_FWD, x_dev[0])
-        out_arrived(out_piece(1, 1 - c), O_OTHER + 1)
-        out_push(out_piece(1, 1 - c), O_FWD + 1, x_dev[1])
+
+    def out_left(n):
+        out_arrived(out_piece(1, 1 - c, n), O_OTHER + 2 * n + 1)
+        out_push(out_piece(1, 1 - c, n), O_FWD + 1 + n, x_dev[1])
 
     def out_end():
         out_arrived(out_piece(1, c), O_OWN + 1)
-        out_arrived(out_piece(-1, 1 - c), O_OTHER)
         out_arrived(out_piece(2, c), O_FWD)
-        out_arrived(out_piece(2, 1 - c), O_FWD + 1)
+        for n in range(2):
+            out_arrived(out_piece(-1, 1 - c, n), O_OTHER + 2 * n)
+            out_arrived(out_piece(2, 1 - c, n), O_FWD + 1 + n)
 
     steps = dict(
         a=share_own,
@@ -515,7 +559,7 @@
         v=weight_out,
         x=weight_out_last,
         s=start_dispatch,
-        w=lambda n: (combine, out_other, out_far, out_end)[n](),
+        w=lambda n, *half: (combine, out_other, out_right, out_left, out_end)[n](*half),
     )
     for word in PLAN:
         steps[word[0]](*(int(n) for n in word[1:]))
@@ -579,8 +623,8 @@
             pltpu.VMEM((NZ, 2, SLOTS, HALF), BF16),
             pltpu.VMEM((NZ, 2, SLOTS, HALF), BF16),
             pltpu.VMEM((2 * NZ, SLOTS, HALF), BF16),
-            pltpu.SemaphoreType.DMA((NZ, COPIES)),
-            pltpu.SemaphoreType.DMA((NZ, COPIES)),
+            pltpu.SemaphoreType.DMA((NZ + 1, COPIES)),
+            pltpu.SemaphoreType.DMA((NZ + 1, COPIES)),
             pltpu.SemaphoreType.DMA((OUT_COPIES,)),
             pltpu.SemaphoreType.DMA((OUT_COPIES,)),
             pltpu.SemaphoreType.DMA((4,)),

time: 150 us -> 148 us (0.987)
  Pallas kernels: 147 us -> 145 us
where the time goes in v4:
time: 148 us
  Pallas kernels  145 us (98%)
    pallas_call x1, Pallas kernels, on_device(): pl.pallas_call(kernel, out_shape=(pltpu.VMEM(layer_inputs.shape, BF16), p...  143 us

profile of v4, /device:TPU:1, one launch (start us, length us, event | category | flops | bytes accessed | tf_op | source)
XLA Modules:
  0.0 147.7 jit_solution(12327550674501029186)
XLA Ops:
  0.6 0.0 copy-start
  0.6 0.7 copy-done
  1.3 0.0 copy-start.1
  1.3 0.7 copy-done.1
  2.0 143.5 %shard_map.85 = (bf16[128,3072]{1,0:T(8,128)(2,1)S(1)}, bf16[768,1024]{1,0:T(8,128)(2,1)S(1)}, bf16[1024,768]{1,0:T(8,128)(2,1)S(1)}) custom-call(bf16[128,3072]{1,0:T(8,128)(2,1)} %x_ref.1, bf16[128,3072]{1,0:T(8,128)(2,1)} %up_ref.1, s32[2,128]{1,0:T(2,128)S(1)} %bitcast.6, f32[2,128]{1,0:T(2,128)S(1)} %bitcast.7, bf16[768,1024]{1,0:T(8,128)(2,1)} %bitcast.8, ...), custom_call_target="tpu_custom_call" | custom-call | flops 12079595520 | bytes 8388608 | tf_op jit(solution)/shard_map/pallas_call | solution.py:605
  145.5 2.0 %shard_map.86 = (bf16[128,3072]{1,0:T(8,128)(2,1)}, bf16[768,1024]{1,0:T(8,128)(2,1)}, bf16[1024,768]{1,0:T(8,128)(2,1)}) custom-call(bf16[128,3072]{1,0:T(8,128)(2,1)S(1)} %get-tuple-element.9.refs_0_, bf16[768,1024]{1,0:T(8,128)(2,1)S(1)} %get-tuple-element.10.refs_1_, bf16[1024,768]{1,0:T(8,128)(2,1)S(1)} %get-tuple-element.11.refs_2_), custom_call_target="tpu_custom_call" | custom-call | bytes 3932160 | tf_op jit(solution)/shard_map/pallas_call | solution.py:588
Async XLA Ops:
  0.6 0.7 copy-start
  1.3 0.7 copy-start.1
